TPU v7x, 128 devices: a whole 4x4x4 slice. The times are simulated.
128 devices in a mesh: island: 8 (over z, core), seq: 16 (over y, x).
Axes of the slice: x: 4, y: 4, z: 4, core: 2. Of those that a mesh axis runs over, the one named last changes fastest.
Arguments:
- query: bfloat16 [32768, 2560], P(('island', 'seq')), parts along dimension 0, may hold values from -6 to 6
- key: bfloat16 [32768, 512], P(('island', 'seq')), parts along dimension 0, may hold values from -6 to 6
- value: bfloat16 [32768, 512], P(('island', 'seq')), parts along dimension 0, may hold values from -6 to 6
- attn_out: bfloat16 [32768, 2560], P(('island', 'seq')), parts along dimension 0, may hold values from -6 to 6
- out_grad: bfloat16 [32768, 2560], P(('island', 'seq')), parts along dimension 0, may hold values from -6 to 6
- log_sums: float32 [20, 32768], P(None, ('island', 'seq')), parts along dimension 1, may hold values from 5 to 8
- block_order: int32 [256], P('island'), parts along dimension 0, may hold values from 0 to 31, each once
- doc_lengths: int32 [32], P('island'), parts along dimension 0, may hold values from 1 to 2048, 4096 in all
Outputs:
- query_grad: bfloat16 [32768, 2560], P(('island', 'seq')), parts along dimension 0
- key_grad: bfloat16 [32768, 512], P(('island', 'seq')), parts along dimension 0
- value_grad: bfloat16 [32768, 512], P(('island', 'seq')), parts along dimension 0
There are 8 independent parts, one for each index of `island`. A program takes and returns all parts, laid end to end along the dimension named above; each array names one. Nothing has to cross between parts.
Inputs may be any that keep to these rules, and one draw needn't show every extreme that they name: `block_order`: every number appears once. `doc_lengths`: the lengths sum to 4096 and the largest is exactly 2048.
All inputs are finite; a program needn't handle non-finite values.
Results may differ from a plain program's by a relative error of at most 0.006.
Values may be sent and summed in bfloat16 or wider, within the bound.
A program may use at most 128 MiB of HBM per device.

v0:
```python
import math

import jax
import jax.numpy as jnp
from jax import lax
from jax.sharding import PartitionSpec as P

HD = 128
BLK = 128


def layout(block_order, doc_lengths):
    count = block_order.shape[0]
    offsets = jnp.tile(jnp.arange(BLK, dtype=jnp.int32), count)
    seq_pos = jnp.repeat(block_order, BLK) * BLK + offsets
    ends = jnp.cumsum(doc_lengths)
    doc_ids = jnp.sum((ends[None, :] <= seq_pos[:, None]).astype(jnp.int32), axis=1)
    return (seq_pos, doc_ids)


def tile_terms(context, keys, values, key_pos, key_doc):
    queries, grads_out, sums, delta, query_pos, query_doc = context
    rows = queries.shape[0]
    span = keys.shape[0]
    groups = keys.shape[1] // HD
    per_group = queries.shape[1] // (groups * HD)
    scale = 1.0 / math.sqrt(HD)
    query_heads = queries.reshape(rows, groups, per_group, HD)
    grad_heads = grads_out.reshape(rows, groups, per_group, HD)
    key_heads = keys.reshape(span, groups, HD)
    value_heads = values.reshape(span, groups, HD)
    allowed = (query_doc[:, None] == key_doc[None, :]) & (key_pos[None, :] <= query_pos[:, None])
    query_shape = (rows, queries.shape[1])
    key_shape = (span, 2 * keys.shape[1])

    def compute(operand):
        scores = (
            jnp.einsum("rgjd,kgd->gjrk", query_heads, key_heads, preferred_element_type=jnp.float32)
            * scale
        )
        probs = jnp.where(allowed, jnp.exp(scores - sums[..., None]), 0.0)
        dprobs = jnp.einsum(
            "rgjd,kgd->gjrk", grad_heads, value_heads, preferred_element_type=jnp.float32
        )
        dscores = (probs * (dprobs - delta[..., None])).astype(jnp.bfloat16)
        query_part = jnp.einsum(
            "gjrk,kgd->rgjd", dscores, key_heads, preferred_element_type=jnp.float32
        ).reshape(query_shape)
        key_part = (
            jnp.einsum(
                "gjrk,rgjd->kgd", dscores, query_heads, preferred_element_type=jnp.float32
            ).reshape(span, -1)
            * scale
        )
        probs_low = probs.astype(jnp.bfloat16)
        value_part = jnp.einsum(
            "gjrk,rgjd->kgd", probs_low, grad_heads, preferred_element_type=jnp.float32
        ).reshape(span, -1)
        key_terms = jnp.concatenate([key_part, value_part], axis=1)
        return (query_part, key_terms)

    def nothing(operand):
        return (jnp.zeros(query_shape, jnp.float32), jnp.zeros(key_shape, jnp.float32))

    return lax.cond(jnp.any(allowed), compute, nothing, 0)


def sweep(context, source, src_begin, pos_begin, length, key_pos_all, key_doc_all):
    width = source.shape[1] // 2
    rows = context[0].shape[0]
    step = math.gcd(length, 512)

    def advance(query_acc, number):
        offset = number * step
        block = lax.dynamic_slice_in_dim(source, src_begin + offset, step, 0)
        key_pos = lax.dynamic_slice_in_dim(key_pos_all, pos_begin + offset, step, 0)
        key_doc = lax.dynamic_slice_in_dim(key_doc_all, pos_begin + offset, step, 0)
        query_part, key_terms = tile_terms(
            context, block[:, :width], block[:, width:], key_pos, key_doc
        )
        return (query_acc + query_part, key_terms)

    start_acc = jnp.zeros((rows, context[0].shape[1]), jnp.float32)
    query_acc, key_terms = lax.scan(advance, start_acc, jnp.arange(length // step, dtype=jnp.int32))
    key_terms = key_terms.reshape(length, -1)
    return (query_acc, key_terms)


def body(query, key, value, attn_out, out_grad, log_sums, block_order, doc_lengths):
    rows = query.shape[0]
    width = key.shape[1]
    groups = width // HD
    per_group = query.shape[1] // (groups * HD)
    scale = 1.0 / math.sqrt(HD)
    key_pos_all, key_doc_all = layout(block_order, doc_lengths)
    total = key_pos_all.shape[0]
    heads = groups * per_group
    delta_flat = jnp.einsum(
        "rhd,rhd->hr",
        out_grad.reshape(rows, heads, HD),
        attn_out.reshape(rows, heads, HD),
        preferred_element_type=jnp.float32,
    )
    first = lax.axis_index("seq") * rows
    query_pos = lax.dynamic_slice_in_dim(key_pos_all, first, rows, 0)
    query_doc = lax.dynamic_slice_in_dim(key_doc_all, first, rows, 0)
    delta = delta_flat.reshape(groups, per_group, rows)
    sums = log_sums.reshape(groups, per_group, rows)
    context = (query, out_grad, sums, delta, query_pos, query_doc)
    joined = jnp.concatenate([key, value], axis=1)
    whole = lax.all_gather(joined, "seq", axis=0, tiled=True)
    query_acc, partial_value = sweep(context, whole, 0, 0, total, key_pos_all, key_doc_all)
    grads = lax.psum_scatter(partial_value, "seq", scatter_dimension=0, tiled=True)
    query_grad = (query_acc * scale).astype(jnp.bfloat16)
    return (
        query_grad,
        grads[:, :width].astype(jnp.bfloat16),
        grads[:, width:].astype(jnp.bfloat16),
    )


def solution(mesh):
    return jax.shard_map(
        body,
        mesh=mesh,
        in_specs=(
            P(("island", "seq"), None),
            P(("island", "seq"), None),
            P(("island", "seq"), None),
            P(("island", "seq"), None),
            P(("island", "seq"), None),
            P(None, ("island", "seq")),
            P("island"),
            P("island"),
        ),
        out_specs=(
            P(("island", "seq"), None),
            P(("island", "seq"), None),
            P(("island", "seq"), None),
        ),
        check_vma=False,
    )
```

profile of v0, /device:TPU:0, one launch (start us, length us, event | category | flops | bytes accessed | tf_op | source)
XLA Modules:
  0.0 418.3 jit_solution(2814217073969200809)
XLA Ops:
  13.9 1.6 copy.73
  15.5 1.7 fusion.11
  17.3 74.0 %all-gather.2.cloned.1.call-done = bf16[4096,1024]{0,1:T(8,128)(2,1)} async-done(((bf16[256,1024]{0,1:T(8,128)(2,1)}), bf16[4096,1024]{0,1:T(8,128)(2,1)}) %all-gather.2.cloned.1.call-update) | async-done | bytes 8388624 | tf_op jit(solution)/shard_map/all_gather | solution.py:111
  91.3 179.1 %while.13 = (s32[]{:T(128)}, f32[256,2560]{0,1:T(8,128)}, f32[8,512,1024]{2,1,0:T(8,128)}, s32[256]{0:T(256)S(1)}, s32[8]{0:T(128)S(1)}, /*index=5*/s32[4096]{0:...) while((s32[]{:T(128)}, f32[256,2560]{0,1:T(8,128)}, ...), condition=%wide.region_6.7_spmd.clone, body=%wide.region_2.6_spmd.clone.sunk | while | flops 3384279040 | bytes 87058800 | solution.py:84
  94.2 16.3 %conditional.3 = (f32[256,2560]{0,1:T(8,128)S(1)}, f32[1,512,1024]{1,2,0:T(8,128)}) conditional(s32[]{:T(128)} %convert_element_type.28, () %tuple.50, (pred[256,512]{0,1:T(8,128)(4,1)S(1)}, bf16[4096,1024]{0,1:T(8,128)(2,1)}, s32[]{:T(128)}, bf16[256,2560]{0,1:T(8,128)(2,1)}, f32[20,256]{1,0:T(8,128)S(1)}, /*index=5*/bf16[256,2560]{0,1:T(8,128)(2,1)}, ...), branch_computations={%region_4.4_spmd, %region_5.5_spmd} | conditional | flops 3382444032 | bytes 70660160 | solution.py:65
  94.2 2.0 fusion.13
  96.2 1.6 fusion.15
  97.8 3.6 fusion.5
  101.4 4.9 %fusion.1 = bf16[4,5,256,512]{2,3,1,0:T(8,128)(2,1)S(1)} fusion(f32[4,512,256,5]{2,1,3,0:T(8,128)S(1)} %fusion.15, f32[4,5,256]{2,1,0:T(8,128)S(1)} %sub.23, f32[4,5,256]{2,1,0:T(8,128)S(1)} %sub.20, pred[256,512]{0,1:T(8,128)(4,1)S(1)} %get-tuple-element.90, bf16[512,4,128,1]{0,2,3,1:T(8,128)(2,1)S(1)} %bitcast.85, bf16[256,4,5,128]{0,3,2,1:T(8,128)(2,1)} %bitcast.8), kind=kOutput, calls=%fused_computation.2 | convolution fusion | flops 686817280 | bytes 17735680 | tf_op jit(solution)/shard_map/while/body/eval_jaxpr/cond/branch_1_fun/rgjd,kgd->gjrk/dot_general | solution.py:42
  106.2 1.8 fusion.8
  110.5 1.9 select_add_fusion.2
  112.4 1.9 copy.78
  118.7 16.3 %conditional.3 = (f32[256,2560]{0,1:T(8,128)S(1)}, f32[1,512,1024]{1,2,0:T(8,128)}) conditional(s32[]{:T(128)} %convert_element_type.28, () %tuple.50, (pred[256,512]{0,1:T(8,128)(4,1)S(1)}, bf16[4096,1024]{0,1:T(8,128)(2,1)}, s32[]{:T(128)}, bf16[256,2560]{0,1:T(8,128)(2,1)}, f32[20,256]{1,0:T(8,128)S(1)}, /*index=5*/bf16[256,2560]{0,1:T(8,128)(2,1)}, ...), branch_computations={%region_4.4_spmd, %region_5.5_spmd} | conditional | flops 3382444032 | bytes 70660160 | solution.py:65
  118.7 2.0 fusion.13
  120.7 1.6 fusion.15
  122.3 3.6 fusion.5
  125.9 4.9 %fusion.1 = bf16[4,5,256,512]{2,3,1,0:T(8,128)(2,1)S(1)} fusion(f32[4,512,256,5]{2,1,3,0:T(8,128)S(1)} %fusion.15, f32[4,5,256]{2,1,0:T(8,128)S(1)} %sub.23, f32[4,5,256]{2,1,0:T(8,128)S(1)} %sub.20, pred[256,512]{0,1:T(8,128)(4,1)S(1)} %get-tuple-element.90, bf16[512,4,128,1]{0,2,3,1:T(8,128)(2,1)S(1)} %bitcast.85, bf16[256,4,5,128]{0,3,2,1:T(8,128)(2,1)} %bitcast.8), kind=kOutput, calls=%fused_computation.2 | convolution fusion | flops 686817280 | bytes 17735680 | tf_op jit(solution)/shard_map/while/body/eval_jaxpr/cond/branch_1_fun/rgjd,kgd->gjrk/dot_general | solution.py:42
  130.7 1.8 fusion.8
  135.0 3.6 select_add_fusion.2
  138.6 1.9 copy.78
  144.9 16.3 %conditional.3 = (f32[256,2560]{0,1:T(8,128)S(1)}, f32[1,512,1024]{1,2,0:T(8,128)}) conditional(s32[]{:T(128)} %convert_element_type.28, () %tuple.50, (pred[256,512]{0,1:T(8,128)(4,1)S(1)}, bf16[4096,1024]{0,1:T(8,128)(2,1)}, s32[]{:T(128)}, bf16[256,2560]{0,1:T(8,128)(2,1)}, f32[20,256]{1,0:T(8,128)S(1)}, /*index=5*/bf16[256,2560]{0,1:T(8,128)(2,1)}, ...), branch_computations={%region_4.4_spmd, %region_5.5_spmd} | conditional | flops 3382444032 | bytes 70660160 | solution.py:65
  144.9 2.0 fusion.13
  146.9 1.6 fusion.15
  148.5 3.6 fusion.5
  152.1 4.9 %fusion.1 = bf16[4,5,256,512]{2,3,1,0:T(8,128)(2,1)S(1)} fusion(f32[4,512,256,5]{2,1,3,0:T(8,128)S(1)} %fusion.15, f32[4,5,256]{2,1,0:T(8,128)S(1)} %sub.23, f32[4,5,256]{2,1,0:T(8,128)S(1)} %sub.20, pred[256,512]{0,1:T(8,128)(4,1)S(1)} %get-tuple-element.90, bf16[512,4,128,1]{0,2,3,1:T(8,128)(2,1)S(1)} %bitcast.85, bf16[256,4,5,128]{0,3,2,1:T(8,128)(2,1)} %bitcast.8), kind=kOutput, calls=%fused_computation.2 | convolution fusion | flops 686817280 | bytes 17735680 | tf_op jit(solution)/shard_map/while/body/eval_jaxpr/cond/branch_1_fun/rgjd,kgd->gjrk/dot_general | solution.py:42
  156.9 1.8 fusion.8
  161.2 3.6 select_add_fusion.2
  164.8 1.9 copy.78
  171.1 1.8 conditional.3
  171.1 1.6 broadcast_in_dim.25
  172.9 3.7 select_add_fusion.2
  176.6 1.9 copy.78
  182.9 16.3 %conditional.3 = (f32[256,2560]{0,1:T(8,128)S(1)}, f32[1,512,1024]{1,2,0:T(8,128)}) conditional(s32[]{:T(128)} %convert_element_type.28, () %tuple.50, (pred[256,512]{0,1:T(8,128)(4,1)S(1)}, bf16[4096,1024]{0,1:T(8,128)(2,1)}, s32[]{:T(128)}, bf16[256,2560]{0,1:T(8,128)(2,1)}, f32[20,256]{1,0:T(8,128)S(1)}, /*index=5*/bf16[256,2560]{0,1:T(8,128)(2,1)}, ...), branch_computations={%region_4.4_spmd, %region_5.5_spmd} | conditional | flops 3382444032 | bytes 70660160 | solution.py:65
  182.9 2.0 fusion.13
  184.9 1.6 fusion.15
  186.5 3.6 fusion.5
  190.1 4.9 %fusion.1 = bf16[4,5,256,512]{2,3,1,0:T(8,128)(2,1)S(1)} fusion(f32[4,512,256,5]{2,1,3,0:T(8,128)S(1)} %fusion.15, f32[4,5,256]{2,1,0:T(8,128)S(1)} %sub.23, f32[4,5,256]{2,1,0:T(8,128)S(1)} %sub.20, pred[256,512]{0,1:T(8,128)(4,1)S(1)} %get-tuple-element.90, bf16[512,4,128,1]{0,2,3,1:T(8,128)(2,1)S(1)} %bitcast.85, bf16[256,4,5,128]{0,3,2,1:T(8,128)(2,1)} %bitcast.8), kind=kOutput, calls=%fused_computation.2 | convolution fusion | flops 686817280 | bytes 17735680 | tf_op jit(solution)/shard_map/while/body/eval_jaxpr/cond/branch_1_fun/rgjd,kgd->gjrk/dot_general | solution.py:42
  194.9 1.8 fusion.8
  199.2 3.6 select_add_fusion.2
  202.8 1.9 copy.78
  209.1 1.8 conditional.3
  209.1 1.6 broadcast_in_dim.25
  210.9 3.7 select_add_fusion.2
  214.6 1.9 copy.78
  220.9 16.3 %conditional.3 = (f32[256,2560]{0,1:T(8,128)S(1)}, f32[1,512,1024]{1,2,0:T(8,128)}) conditional(s32[]{:T(128)} %convert_element_type.28, () %tuple.50, (pred[256,512]{0,1:T(8,128)(4,1)S(1)}, bf16[4096,1024]{0,1:T(8,128)(2,1)}, s32[]{:T(128)}, bf16[256,2560]{0,1:T(8,128)(2,1)}, f32[20,256]{1,0:T(8,128)S(1)}, /*index=5*/bf16[256,2560]{0,1:T(8,128)(2,1)}, ...), branch_computations={%region_4.4_spmd, %region_5.5_spmd} | conditional | flops 3382444032 | bytes 70660160 | solution.py:65
  220.9 2.0 fusion.13
  222.9 1.6 fusion.15
  224.5 3.6 fusion.5
  228.1 4.9 %fusion.1 = bf16[4,5,256,512]{2,3,1,0:T(8,128)(2,1)S(1)} fusion(f32[4,512,256,5]{2,1,3,0:T(8,128)S(1)} %fusion.15, f32[4,5,256]{2,1,0:T(8,128)S(1)} %sub.23, f32[4,5,256]{2,1,0:T(8,128)S(1)} %sub.20, pred[256,512]{0,1:T(8,128)(4,1)S(1)} %get-tuple-element.90, bf16[512,4,128,1]{0,2,3,1:T(8,128)(2,1)S(1)} %bitcast.85, bf16[256,4,5,128]{0,3,2,1:T(8,128)(2,1)} %bitcast.8), kind=kOutput, calls=%fused_computation.2 | convolution fusion | flops 686817280 | bytes 17735680 | tf_op jit(solution)/shard_map/while/body/eval_jaxpr/cond/branch_1_fun/rgjd,kgd->gjrk/dot_general | solution.py:42
  232.9 1.8 fusion.8
  237.2 3.6 select_add_fusion.2
  240.8 1.9 copy.78
  247.1 16.2 %conditional.3 = (f32[256,2560]{0,1:T(8,128)S(1)}, f32[1,512,1024]{1,2,0:T(8,128)}) conditional(s32[]{:T(128)} %convert_element_type.28, () %tuple.50, (pred[256,512]{0,1:T(8,128)(4,1)S(1)}, bf16[4096,1024]{0,1:T(8,128)(2,1)}, s32[]{:T(128)}, bf16[256,2560]{0,1:T(8,128)(2,1)}, f32[20,256]{1,0:T(8,128)S(1)}, /*index=5*/bf16[256,2560]{0,1:T(8,128)(2,1)}, ...), branch_computations={%region_4.4_spmd, %region_5.5_spmd} | conditional | flops 3382444032 | bytes 70660160 | solution.py:65
  247.1 1.9 fusion.13
  249.1 1.6 fusion.15
  250.6 3.6 fusion.5
  254.2 4.9 %fusion.1 = bf16[4,5,256,512]{2,3,1,0:T(8,128)(2,1)S(1)} fusion(f32[4,512,256,5]{2,1,3,0:T(8,128)S(1)} %fusion.15, f32[4,5,256]{2,1,0:T(8,128)S(1)} %sub.23, f32[4,5,256]{2,1,0:T(8,128)S(1)} %sub.20, pred[256,512]{0,1:T(8,128)(4,1)S(1)} %get-tuple-element.90, bf16[512,4,128,1]{0,2,3,1:T(8,128)(2,1)S(1)} %bitcast.85, bf16[256,4,5,128]{0,3,2,1:T(8,128)(2,1)} %bitcast.8), kind=kOutput, calls=%fused_computation.2 | convolution fusion | flops 686817280 | bytes 17735680 | tf_op jit(solution)/shard_map/while/body/eval_jaxpr/cond/branch_1_fun/rgjd,kgd->gjrk/dot_general | solution.py:42
  259.1 1.8 fusion.8
  263.3 3.6 select_add_fusion.2
  267.0 1.9 copy.78
  270.4 1.7 copy-done.1
  272.1 2.1 copy.49
  274.2 3.0 multiply_convert_fusion
  277.2 132.2 %reduce-scatter.2.cloned.1.call-done = f32[256,1024]{1,0:T(8,128)} async-done(((f32[4096,1024]{1,0:T(8,128)}), f32[256,1024]{1,0:T(8,128)}) %reduce-scatter.2.cloned.1.call-update) | async-done | bytes 1048592 | tf_op jit(solution)/shard_map/reduce_scatter | solution.py:113
  (109 shorter events, 48.1 us)
Async XLA Ops:
  7.2 3.4 copy-start.5
  7.2 3.5 copy-start.6
  7.2 3.9 copy-start.2
  7.2 5.3 %copy-start.3 = (bf16[256,2560]{1,0:T(8,128)(2,1)S(1)}, bf16[256,2560]{1,0:T(8,128)(2,1)}, u32[]{:S(2)}) copy-start(bf16[256,2560]{1,0:T(8,128)(2,1)} %param.12) | copy-start | bytes 3932164
  7.2 84.1 %all-gather.2.cloned.1.call-start = ((), (), s32[]{:S(2)}) async-start(), calls=%async_computation.1 | async-start | bytes 8912896 | tf_op jit(solution)/shard_map/all_gather | solution.py:111
  10.4 398.9 %reduce-scatter.2.cloned.1.call-start = ((), (), s32[]{:S(2)}) async-start(), calls=%async_computation.2 | async-start | bytes 17825792 | tf_op jit(solution)/shard_map/reduce_scatter | solution.py:113
  13.9 77.3 %copy-start.4 = (f32[20,256]{1,0:T(8,128)S(1)}, f32[20,256]{1,0:T(8,128)}, u32[]{:S(2)}) copy-start(f32[20,256]{1,0:T(8,128)} %param.17) | copy-start | bytes 61444
  94.2 2.0 copy-start
  118.7 2.0 copy-start
  144.9 2.0 copy-start
  182.9 2.0 copy-start
  220.9 2.0 copy-start
  247.1 1.9 copy-start
  270.3 1.7 copy-start.1
Sparse Core Ops, SparseCore 0:
  10.6 80.6 all-gather.1
  270.5 138.7 reduce-scatter.1
where the time goes:
time: 420 us; the launch traced here: 418 us
  waiting for transfers between devices  206 us (49%)
  matrix products  76.1 us (18%)
  local copies, waits for them, and re-layouts  60 us (14%)
  other arithmetic  50.8 us (12%)
  between operations  14.2 us (3%)
  loops' own time  11.1 us (3%)
    reduce_scatter x1, waiting for transfers between devices, body(): lax.psum_scatter(partial_value, 'seq', scatter_dimension=0, tiled=True)  132 us
    all_gather x1, waiting for transfers between devices, body(): whole = lax.all_gather(joined, 'seq', axis=0, tiled=True)  74 us
    dot_general x6, matrix products, compute(): jnp.einsum('rgjd,kgd->gjrk', grad_heads, value_heads, preferred_element_t...  29.1 us
    add x8, other arithmetic, advance(): return (query_acc + query_part, key_terms)  27.4 us
    dynamic_update_slice x16, local copies, waits for them, and re-layouts, sweep(): lax.scan(advance, start_acc, jnp.arange(length // step, dtype=jnp.int32))  27.1 us
    dot_general x6, matrix products, compute(): jnp.einsum('gjrk,rgjd->kgd', probs_low, grad_heads, preferred_element_typ...  21.6 us
    slice x6, local copies, waits for them, and re-layouts, advance(): block[:, width:]  11.7 us
    dot_general x6, matrix products, compute(): jnp.einsum('gjrk,rgjd->kgd', dscores, query_heads, preferred_element_type...  10.9 us
  transfers between devices with their start and end apart: 2, of which 2 were waited for; matrix products, arithmetic and copies ran while one was open for 3% of the time, Pallas kernels for 0%

commit v1 on v0

v1 whole, which is shorter than its diff:
```python
import functools
import math

import jax
import jax.numpy as jnp
from jax import lax
from jax.experimental import pallas as pl
from jax.experimental.pallas import tpu as pltpu
from jax.sharding import PartitionSpec as P

MESH = pl.DeviceIdType.MESH
HD = 128
BLK = 128
SIDE = 4
ROWS = 256
GROUP = 5
QW = GROUP * HD
TOKENS = 4096
NBLK = 32
STEP = 256
PAD = STEP - BLK
SCALE = 1.0 / math.sqrt(HD)
LOG2E = math.log2(math.e)
NT = (((1,), (1,)), ((), ()))
TN = (((0,), (0,)), ((), ()))


def place():
    core = lax.rem(lax.axis_index("island"), 2)
    seq = lax.axis_index("seq")
    x, y = lax.rem(seq, SIDE), seq // SIDE
    a = x + core * (y - x)
    b = y + core * (x - y)
    return a, b, 1 + 3 * core, SIDE - 3 * core


class Wires:
    def __init__(self, send_sems, recv_sems):
        self.send_sems, self.recv_sems, self.count = send_sems, recv_sems, 0

    def send(self, src, dst, device):
        n = self.count
        self.count += 1
        copy = pltpu.make_async_remote_copy(
            src, dst, self.send_sems.at[n], self.recv_sems.at[n], device_id=device, device_id_type=MESH
        )
        copy.start()
        return copy


def span(start, size):
    return pl.ds(pl.multiple_of(start * size, size), size)


def greet(devices):
    barrier = pltpu.get_barrier_semaphore()
    for device in devices:
        pl.semaphore_signal(barrier, inc=1, device_id=device, device_id_type=MESH)
    pl.semaphore_wait(barrier, len(devices))


def gather_kernel(
    q_ref, k_ref, v_ref, o_ref, do_ref, lse_ref, qx, dox, kv, auxx, o_buf, do_buf, aux, ssem, rsem, lsem
):
    a, b, sa, sb = place()
    A = [lax.rem(a + t, SIDE) for t in range(SIDE)]
    B = [lax.rem(b + t, SIDE) for t in range(SIDE)]

    def dev(aa, bb):
        return {"seq": aa * sa + bb * sb}

    def slot(aa, bb):
        return span(aa * sa + bb * sb, ROWS)

    loads = [
        pltpu.make_async_copy(o_ref, o_buf, lsem.at[0]),
        pltpu.make_async_copy(do_ref, do_buf, lsem.at[1]),
    ]
    for load in loads:
        load.start()
    greet([dev(A[1], b), dev(A[3], b), dev(A[2], b), dev(a, B[1]), dev(a, B[3])])
    wires = Wires(ssem, rsem)
    mine = slot(a, b)
    first = {}
    for t in (1, 3, 2):
        first[t] = [
            wires.send(s.at[:, span(A[t], HD)], kv.at[mine, pl.ds(n * HD, HD)], dev(A[t], b))
            for n, s in enumerate((k_ref, v_ref))
        ]
    local = [
        pltpu.make_async_copy(k_ref.at[:, span(a, HD)], kv.at[mine, pl.ds(0, HD)], lsem.at[2]),
        pltpu.make_async_copy(v_ref.at[:, span(a, HD)], kv.at[mine, pl.ds(HD, HD)], lsem.at[3]),
        pltpu.make_async_copy(q_ref.at[:, span(a, QW)], qx.at[span(a, ROWS)], lsem.at[4]),
        pltpu.make_async_copy(do_ref.at[:, span(a, QW)], dox.at[span(a, ROWS)], lsem.at[5]),
    ]
    for copy in local:
        copy.start()
    rest = []
    for t in (1, 3, 2):
        for s, d in ((q_ref, qx), (do_ref, dox)):
            rest.append(wires.send(s.at[:, span(A[t], QW)], d.at[span(a, ROWS)], dev(A[t], b)))

    passed = {}

    def spread(t):
        rows = slot(A[t], b)
        passed[t] = (
            wires.send(kv.at[rows], kv.at[rows], dev(a, B[1])),
            wires.send(kv.at[rows], kv.at[rows], dev(a, B[3])),
        )

    local[0].wait()
    local[1].wait()
    spread(0)
    for t in (1, 3, 2):
        for copy in first[SIDE - t]:
            copy.wait_recv()
        spread(t)

    for load in loads:
        load.wait()
    ones = jnp.ones((8, HD), jnp.bfloat16)
    aux[...] = jnp.zeros_like(aux)
    for g in range(SIDE):
        for h in range(GROUP):
            n = g * GROUP + h
            cols = slice(n * HD, (n + 1) * HD)
            prod = o_buf[:, cols].astype(jnp.float32) * do_buf[:, cols].astype(jnp.float32)
            high = prod.astype(jnp.bfloat16)
            low = (prod - high.astype(jnp.float32)).astype(jnp.bfloat16)
            delta = lax.dot_general(ones, high, NT, preferred_element_type=jnp.float32)
            delta += lax.dot_general(ones, low, NT, preferred_element_type=jnp.float32)
            aux[g, h : h + 1, :] = lse_ref[n : n + 1, :] * LOG2E
            aux[g, 8 + h : 9 + h, :] = delta[0:1]
    for t in (1, 3, 2):
        rest.append(wires.send(aux.at[A[t]], auxx.at[a], dev(A[t], b)))
    own = pltpu.make_async_copy(aux.at[a], auxx.at[a], lsem.at[6])
    own.start()

    second = []
    for t in (0, 1, 3, 2):
        up, down = passed[t]
        up.wait_recv()
        if t in (0, 1):
            rows = slot(A[t], B[3])
            second.append(wires.send(kv.at[rows], kv.at[rows], dev(a, B[1])))
        down.wait_recv()
        if t in (2, 3):
            rows = slot(A[t], B[1])
            second.append(wires.send(kv.at[rows], kv.at[rows], dev(a, B[3])))
    for copy in rest + second:
        copy.wait()
    for t in (1, 3, 2):
        for copy in first[t]:
            copy.wait_send()
    for t in range(SIDE):
        for copy in passed[t]:
            copy.wait_send()
    for copy in local[2:] + [own]:
        copy.wait()


def attend_kernel(
    order, docs, qx, dox, aux, kv, dq_ref, dkv_ref, keys, acc, qs, dos, dqt, inverse, sems
):
    a, b, sa, sb = place()

    def invert(n, carry):
        inverse[order[n]] = n
        return carry

    lax.fori_loop(0, NBLK, invert, 0)

    def load(c):
        return pltpu.make_async_copy(
            kv.at[span(inverse[c], BLK)], keys.at[pl.ds(pl.multiple_of(PAD + c * BLK, BLK), BLK)], sems.at[c]
        )

    def start(c, carry):
        load(c).start()
        return carry

    lax.fori_loop(0, NBLK, start, 0)
    keys[0:PAD, :] = jnp.zeros((PAD, 2 * HD), jnp.bfloat16)
    acc[...] = jnp.zeros_like(acc)
    e0 = docs[0]
    e1 = e0 + docs[1]
    e2 = e1 + docs[2]

    def finish(c, carry):
        load(c).wait()
        return carry

    lax.fori_loop(0, NBLK, finish, 0)

    def block(i, carry):
        aa = i // 2
        j = order[(aa * sa + b * sb) * 2 + lax.rem(i, 2)]
        rows = span(i, BLK)
        for h in range(GROUP):
            part = pl.ds(h * BLK, BLK)
            qs[part, :] = qx[rows, h * HD : (h + 1) * HD]
            dos[part, :] = dox[rows, h * HD : (h + 1) * HD]
        tok = pl.ds(pl.multiple_of(lax.rem(i, 2) * BLK, BLK), BLK)
        lse = jnp.concatenate([aux[aa, h : h + 1, tok] for h in range(GROUP)], axis=1)
        delta = jnp.concatenate([aux[aa, 8 + h : 9 + h, tok] for h in range(GROUP)], axis=1)
        pos = j * BLK + lax.broadcasted_iota(jnp.int32, (1, BLK), 1)
        begin = jnp.zeros((1, BLK), jnp.int32)
        low = jnp.int32(0)
        for e in (e0, e1, e2):
            begin = jnp.where(pos >= e, e, begin)
            low = jnp.where(j * BLK >= e, e, low)
        low = low // BLK
        dqt[...] = jnp.zeros_like(dqt)
        steps = (j - low + 1 + STEP // BLK - 1) // (STEP // BLK)

        def step(s, carry2):
            top = j - s * (STEP // BLK)
            at = pl.ds(pl.multiple_of(top * BLK, BLK), STEP)
            k = keys[at, 0:HD]
            v = keys[at, HD : 2 * HD]
            where = top * BLK - PAD + lax.broadcasted_iota(jnp.int32, (STEP, BLK), 0)
            allowed = (where >= begin) & (where <= pos)
            st = lax.dot_general(k, qs[...], NT, preferred_element_type=jnp.float32)
            dpt = lax.dot_general(v, dos[...], NT, preferred_element_type=jnp.float32)
            p_parts, d_parts = [], []
            for h in range(GROUP):
                part = slice(h * BLK, (h + 1) * BLK)
                p = jnp.exp2(st[:, part] * (SCALE * LOG2E) - lse[:, part])
                p = jnp.where(allowed, p, 0.0)
                d = p * (dpt[:, part] - delta[:, part])
                p_parts.append(p.astype(jnp.bfloat16))
                d_parts.append(d.astype(jnp.bfloat16))
            pt = jnp.concatenate(p_parts, axis=1)
            dst = jnp.concatenate(d_parts, axis=1)
            acc[at, HD : 2 * HD] += jnp.dot(pt, dos[...], preferred_element_type=jnp.float32)
            acc[at, 0:HD] += jnp.dot(dst, qs[...], preferred_element_type=jnp.float32)
            dqt[...] += lax.dot_general(k, dst, TN, preferred_element_type=jnp.float32)
            return carry2

        lax.fori_loop(0, steps, step, 0)
        for h in range(GROUP):
            part = dqt[:, h * BLK : (h + 1) * BLK] * SCALE
            dq_ref[rows, h * HD : (h + 1) * HD] = part.T.astype(jnp.bfloat16)
        return carry

    lax.fori_loop(0, 2 * SIDE, block, 0)

    def emit(c, carry):
        dkv_ref[span(inverse[c], BLK), :] = acc[pl.ds(pl.multiple_of(PAD + c * BLK, BLK), BLK), :].astype(
            jnp.bfloat16
        )
        return carry

    lax.fori_loop(0, NBLK, emit, 0)


def scatter_kernel(dqx, dkv, dq, dk, dv, own, mid, thr, got, grads, ssem, rsem, lsem):
    a, b, sa, sb = place()
    A = [lax.rem(a + t, SIDE) for t in range(SIDE)]
    B = [lax.rem(b + t, SIDE) for t in range(SIDE)]

    def dev(aa, bb):
        return {"seq": aa * sa + bb * sb}

    def slot(aa, bb):
        return span(aa * sa + bb * sb, ROWS)

    up, down = dev(a, B[1]), dev(a, B[3])
    toward = (up, up, down, down)
    next_b = (B[1], B[1], B[3], B[3])
    loads = [pltpu.make_async_copy(dkv.at[slot(A[t], next_b[t])], mid.at[t], lsem.at[t]) for t in range(SIDE)]
    loads += [pltpu.make_async_copy(dkv.at[slot(A[t], b)], own.at[t], lsem.at[4 + t]) for t in range(SIDE)]
    for load in loads:
        load.start()
    greet([dev(A[1], b), dev(A[3], b), dev(A[2], b), up, down])
    wires = Wires(ssem, rsem)
    through = [wires.send(dkv.at[slot(A[t], B[2])], thr.at[t], toward[t]) for t in range(SIDE)]
    plain = [None] * SIDE
    for t in (2, 3):
        plain[t] = wires.send(dkv.at[slot(A[t], B[1])], got.at[0, t], up)
    for t in (0, 1):
        plain[t] = wires.send(dkv.at[slot(A[t], B[3])], got.at[1, t], down)
    heads = [
        wires.send(dqx.at[span(A[t], ROWS)], dq.at[:, span(a, QW)], dev(A[t], b)) for t in (1, 3, 2)
    ]
    mine = pltpu.make_async_copy(dqx.at[span(a, ROWS)], dq.at[:, span(a, QW)], lsem.at[8])
    mine.start()
    summed = [None] * SIDE
    for t in (0, 2, 1, 3):
        loads[t].wait()
        through[t].wait_recv()
        total = mid[t].astype(jnp.float32) + thr[t].astype(jnp.float32)
        mid[t] = total.astype(jnp.bfloat16)
        side = 0 if t < 2 else 1
        summed[t] = wires.send(mid.at[t], got.at[side, t], toward[t])
    last = []
    copies = []
    for t in (2, 1, 3, 0):
        loads[4 + t].wait()
        plain[t].wait_recv()
        summed[t].wait_recv()
        total = own[t].astype(jnp.float32) + got[0, t].astype(jnp.float32) + got[1, t].astype(jnp.float32)
        grads[t, :, 0:HD] = (total[:, 0:HD] * SCALE).astype(jnp.bfloat16)
        grads[t, :, HD : 2 * HD] = total[:, HD : 2 * HD].astype(jnp.bfloat16)
        for n, d in enumerate((dk, dv)):
            src = grads.at[t, :, pl.ds(n * HD, HD)]
            if t:
                last.append(wires.send(src, d.at[:, span(a, HD)], dev(A[t], b)))
            else:
                copy = pltpu.make_async_copy(src, d.at[:, span(a, HD)], lsem.at[9 + n])
                copy.start()
                copies.append(copy)
    for copy in heads + last:
        copy.wait()
    for copy in through + plain + summed:
        copy.wait_send()
    for copy in copies + [mine]:
        copy.wait()


def gather_call(query, key, value, attn_out, out_grad, log_sums):
    any_spec = pl.BlockSpec(memory_space=pl.ANY)
    bf = jnp.bfloat16
    return pl.pallas_call(
        gather_kernel,
        out_shape=[
            jax.ShapeDtypeStruct((SIDE * ROWS, QW), bf),
            jax.ShapeDtypeStruct((SIDE * ROWS, QW), bf),
            jax.ShapeDtypeStruct((TOKENS, 2 * HD), bf),
            jax.ShapeDtypeStruct((SIDE, 16, ROWS), jnp.float32),
        ],
        in_specs=[any_spec] * 5 + [pl.BlockSpec(memory_space=pltpu.VMEM)],
        out_specs=[any_spec] * 4,
        scratch_shapes=[
            pltpu.VMEM((ROWS, SIDE * QW), bf),
            pltpu.VMEM((ROWS, SIDE * QW), bf),
            pltpu.VMEM((SIDE, 16, ROWS), jnp.float32),
            pltpu.SemaphoreType.DMA((32,)),
            pltpu.SemaphoreType.DMA((32,)),
            pltpu.SemaphoreType.DMA((8,)),
        ],
        compiler_params=pltpu.CompilerParams(
            collective_id=1, has_side_effects=True, vmem_limit_bytes=24 * 2**20
        ),
        name="gather",
    )(query, key, value, attn_out, out_grad, log_sums)


def attend_call(order, docs, qx, dox, aux, kv):
    bf = jnp.bfloat16
    vmem = pl.BlockSpec(memory_space=pltpu.VMEM)
    smem = pl.BlockSpec(memory_space=pltpu.SMEM)
    return pl.pallas_call(
        attend_kernel,
        out_shape=[
            jax.ShapeDtypeStruct((SIDE * ROWS, QW), bf),
            jax.ShapeDtypeStruct((TOKENS, 2 * HD), bf),
        ],
        in_specs=[smem, smem, vmem, vmem, vmem, pl.BlockSpec(memory_space=pl.ANY)],
        out_specs=[vmem, vmem],
        scratch_shapes=[
            pltpu.VMEM((PAD + TOKENS, 2 * HD), bf),
            pltpu.VMEM((PAD + TOKENS, 2 * HD), jnp.float32),
            pltpu.VMEM((QW, HD), bf),
            pltpu.VMEM((QW, HD), bf),
            pltpu.VMEM((HD, QW), jnp.float32),
            pltpu.SMEM((NBLK,), jnp.int32),
            pltpu.SemaphoreType.DMA((NBLK,)),
        ],
        compiler_params=pltpu.CompilerParams(vmem_limit_bytes=48 * 2**20),
        name="attend",
    )(order, docs, qx, dox, aux, kv)


def scatter_call(dqx, dkv):
    bf = jnp.bfloat16
    any_spec = pl.BlockSpec(memory_space=pl.ANY)
    piece = (SIDE, ROWS, 2 * HD)
    return pl.pallas_call(
        scatter_kernel,
        out_shape=[
            jax.ShapeDtypeStruct((ROWS, SIDE * QW), bf),
            jax.ShapeDtypeStruct((ROWS, SIDE * HD), bf),
            jax.ShapeDtypeStruct((ROWS, SIDE * HD), bf),
        ],
        in_specs=[any_spec] * 2,
        out_specs=[any_spec] * 3,
        scratch_shapes=[
            pltpu.VMEM(piece, bf),
            pltpu.VMEM(piece, bf),
            pltpu.VMEM(piece, bf),
            pltpu.VMEM((2,) + piece, bf),
            pltpu.VMEM(piece, bf),
            pltpu.SemaphoreType.DMA((24,)),
            pltpu.SemaphoreType.DMA((24,)),
            pltpu.SemaphoreType.DMA((12,)),
        ],
        compiler_params=pltpu.CompilerParams(
            collective_id=2, has_side_effects=True, vmem_limit_bytes=24 * 2**20
        ),
        name="scatter",
    )(dqx, dkv)


def body(query, key, value, attn_out, out_grad, log_sums, block_order, doc_lengths):
    qx, dox, kv, aux = gather_call(query, key, value, attn_out, out_grad, log_sums)
    dqx, dkv = attend_call(block_order, doc_lengths, qx, dox, aux, kv)
    return scatter_call(dqx, dkv)


def solution(mesh):
    rows = P(("island", "seq"), None)
    return jax.shard_map(
        body,
        mesh=mesh,
        in_specs=(rows,) * 5 + (P(None, ("island", "seq")), P("island"), P("island")),
        out_specs=(rows,) * 3,
        check_vma=False,
    )
```

time: 420 us -> 98.8 us (0.24)
  waiting for transfers between devices: 206 us -> 0 us
  Pallas kernels: 0 us -> 87 us
  matrix products: 76.1 us -> 0 us
  other arithmetic: 50.8 us -> 0 us
  local copies, waits for them, and re-layouts: 60 us -> 10.4 us
  between operations: 14.2 us -> 0.68 us
  loops' own time: 11.1 us -> 0 us
    reduce_scatter x1 -> x0, waiting for transfers between devices: 132 us -> none  [body(): lax.psum_scatter(partial_value, 'seq', scatter_dimension=0, tiled=True)]
    pallas_call x0 -> x3, Pallas kernels: none -> 87 us  [the longest x1 33.4 us: gather_call(): pl.pallas_call(gather_kernel, out_shape=[jax.ShapeDtypeStruct((SIDE * ROW...]
    dot_general x30 -> x0, matrix products: 76.1 us -> none  [the longest x6 29.1 us: compute(): jnp.einsum('rgjd,kgd->gjrk', grad_heads, value_heads, preferred_element_t...]
    all_gather x1 -> x0, waiting for transfers between devices: 74 us -> none  [body(): whole = lax.all_gather(joined, 'seq', axis=0, tiled=True)]
    add x9 -> x0, other arithmetic: 27.5 us -> none  [the longest x8 27.4 us: advance(): return (query_acc + query_part, key_terms)]
    dynamic_update_slice x16 -> x0, local copies, waits for them, and re-layouts: 27.1 us -> none  [sweep(): lax.scan(advance, start_acc, jnp.arange(length // step, dtype=jnp.int32))]
    slice x7 -> x0, local copies, waits for them, and re-layouts: 12.5 us -> none  [the longest x6 11.7 us: advance(): block[:, width:]]
    another operation x9 -> x0, loops' own time: 11.1 us -> none  [the longest x1 10.5 us: sweep(): lax.scan(advance, start_acc, jnp.arange(length // step, dtype=jnp.int32))]
  transfers between devices with their start and end apart: 2 -> 0, of which waited for: 2 -> 0; matrix products, arithmetic and copies ran while one was open for 3% -> 0% of each run, Pallas kernels for 0% -> 0%
where the time goes in v1:
time: 98.8 us; the launch traced here: 98.1 us
  Pallas kernels  87 us (88%)
  local copies, waits for them, and re-layouts  10.4 us (11%)
    pallas_call x1, Pallas kernels, gather_call(): pl.pallas_call(gather_kernel, out_shape=[jax.ShapeDtypeStruct((SIDE * ROW...  33.4 us
    pallas_call x1, Pallas kernels, scatter_call(): pl.pallas_call(scatter_kernel, out_shape=[jax.ShapeDtypeStruct((ROWS, SID...  30.2 us
    pallas_call x1, Pallas kernels, attend_call(): pl.pallas_call(attend_kernel, out_shape=[jax.ShapeDtypeStruct((SIDE * ROW...  23.4 us
    unnamed x21, local copies, waits for them, and re-layouts  10.4 us

profile of v1, /device:TPU:0, one launch (start us, length us, event | category | flops | bytes accessed | tf_op | source)
XLA Modules:
  0.0 98.1 jit_solution(9411888434670003130)
XLA Ops:
  0.6 0.0 copy-start.1
  0.6 1.3 %copy-done.1 = bf16[256,2560]{1,0:T(8,128)(2,1)S(1)} copy-done((bf16[256,2560]{1,0:T(8,128)(2,1)S(1)}, bf16[256,2560]{1,0:T(8,128)(2,1)}, u32[]{:S(2)}) %copy-start.1) | copy-done | bytes 1310744
  2.0 0.0 copy-start.2
  2.0 1.3 %copy-done.2 = bf16[256,2560]{1,0:T(8,128)(2,1)S(1)} copy-done((bf16[256,2560]{1,0:T(8,128)(2,1)S(1)}, bf16[256,2560]{1,0:T(8,128)(2,1)}, u32[]{:S(2)}) %copy-start.2) | copy-done | bytes 1310744
  3.3 0.0 copy-start.3
  3.3 1.3 %copy-done.3 = bf16[256,2560]{1,0:T(8,128)(2,1)S(1)} copy-done((bf16[256,2560]{1,0:T(8,128)(2,1)S(1)}, bf16[256,2560]{1,0:T(8,128)(2,1)}, u32[]{:S(2)}) %copy-start.3) | copy-done | bytes 1310744
  4.6 0.0 copy-start.4
  4.6 0.9 copy-done.4
  5.5 0.0 copy-start.5
  5.5 0.9 copy-done.5
  6.5 0.0 copy-start.6
  6.5 0.7 copy-done.6
  7.2 0.0 copy-start.7
  7.2 0.0 copy-start.8
  7.2 33.4 %gather.1 = (bf16[1024,640]{1,0:T(8,128)(2,1)S(1)}, bf16[1024,640]{1,0:T(8,128)(2,1)S(1)}, bf16[4096,256]{1,0:T(8,128)(2,1)S(1)}, f32[4,16,256]{2,1,0:T(8,128)S(1)}) custom-call(bf16[256,2560]{1,0:T(8,128)(2,1)S(1)} %copy-done.1, bf16[256,512]{1,0:T(8,128)(2,1)S(1)} %copy-done.4, bf16[256,512]{1,0:T(8,128)(2,1)S(1)} %copy-done.5, ...), custom_call_target="tpu_custom_call" | custom-call | tf_op jit(solution)/shard_map/gather/pallas_call | solution.py:325
  40.6 0.0 copy-start
  40.7 1.3 %copy-done = bf16[4096,256]{1,0:T(8,128)(2,1)} copy-done((bf16[4096,256]{1,0:T(8,128)(2,1)}, bf16[4096,256]{1,0:T(8,128)(2,1)S(1)}, u32[]{:S(2)}) %copy-start) | copy-done | bytes 2097176
  42.0 0.0 copy-done.7
  42.0 0.0 copy-done.8
  42.0 23.4 %attend.1 = (bf16[1024,640]{1,0:T(8,128)(2,1)S(1)}, bf16[4096,256]{1,0:T(8,128)(2,1)S(1)}) custom-call(s32[32]{0:T(128)S(1)} %copy-done.7, s32[4]{0:T(128)S(1)} %copy-done.8, bf16[1024,640]{1,0:T(8,128)(2,1)S(1)} %get-tuple-element.9.qx, bf16[1024,640]{1,0:T(8,128)(2,1)S(1)} %get-tuple-element.10.dox, f32[4,16,256]{2,1,0:T(8,128)S(1)} %get-tuple-element.11.aux, ...), custom_call_target="tpu_custom_call" | custom-call | tf_op jit(solution)/shard_map/attend/pallas_call | solution.py:354
  65.4 30.2 %scatter.1 = (bf16[256,2560]{1,0:T(8,128)(2,1)S(1)}, bf16[256,512]{1,0:T(8,128)(2,1)S(1)}, bf16[256,512]{1,0:T(8,128)(2,1)S(1)}) custom-call(bf16[1024,640]{1,0:T(8,128)(2,1)S(1)} %get-tuple-element.13.dqx, bf16[4096,256]{1,0:T(8,128)(2,1)S(1)} %get-tuple-element.14.dkv), custom_call_target="tpu_custom_call" | custom-call | tf_op jit(solution)/shard_map/scatter/pallas_call | solution.py:380
  95.6 1.1 %copy.14 = bf16[256,2560]{1,0:T(8,128)(2,1)} copy(bf16[256,2560]{1,0:T(8,128)(2,1)S(1)} %get-tuple-element.18) | data formatting | bytes 2621440
  96.7 0.7 copy.15
  97.4 0.7 copy.16
Async XLA Ops:
  0.6 1.3 %copy-start.1 = (bf16[256,2560]{1,0:T(8,128)(2,1)S(1)}, bf16[256,2560]{1,0:T(8,128)(2,1)}, u32[]{:S(2)}) copy-start(bf16[256,2560]{1,0:T(8,128)(2,1)} %q_ref.1) | copy-start | bytes 3932164
  2.0 1.3 %copy-start.2 = (bf16[256,2560]{1,0:T(8,128)(2,1)S(1)}, bf16[256,2560]{1,0:T(8,128)(2,1)}, u32[]{:S(2)}) copy-start(bf16[256,2560]{1,0:T(8,128)(2,1)} %o_ref.1) | copy-start | bytes 3932164
  3.3 1.3 %copy-start.3 = (bf16[256,2560]{1,0:T(8,128)(2,1)S(1)}, bf16[256,2560]{1,0:T(8,128)(2,1)}, u32[]{:S(2)}) copy-start(bf16[256,2560]{1,0:T(8,128)(2,1)} %do_ref.1) | copy-start | bytes 3932164
  4.6 0.9 copy-start.4
  5.5 0.9 copy-start.5
  6.5 0.7 copy-start.6
  7.2 34.8 %copy-start.7 = (s32[32]{0:T(128)S(1)}, s32[32]{0:T(128)}, u32[]{:S(2)}) copy-start(s32[32]{0:T(128)} %order.1) | copy-start | bytes 388
  7.2 34.8 %copy-start.8 = (s32[4]{0:T(128)S(1)}, s32[4]{0:T(128)}, u32[]{:S(2)}) copy-start(s32[4]{0:T(128)} %docs.1) | copy-start | bytes 52
  40.6 1.3 %copy-start = (bf16[4096,256]{1,0:T(8,128)(2,1)}, bf16[4096,256]{1,0:T(8,128)(2,1)S(1)}, u32[]{:S(2)}) copy-start(bf16[4096,256]{1,0:T(8,128)(2,1)S(1)} %get-tuple-element.12.kv) | copy-start | bytes 6291460

commit v2 on v1

v2 whole, which is shorter than its diff:
```python
import functools
import math

import jax
import jax.numpy as jnp
from jax import lax
from jax.experimental import pallas as pl
from jax.experimental.pallas import tpu as pltpu
from jax.sharding import PartitionSpec as P

MESH = pl.DeviceIdType.MESH
HD = 128
BLK = 128
SIDE = 4
ROWS = 256
GROUP = 5
QW = GROUP * HD
TOKENS = 4096
NBLK = 32
PAIR = 2 * BLK
NLOC = 2 * SIDE
SCALE = 1.0 / math.sqrt(HD)
LOG2E = math.log2(math.e)
DEEP = 2
BEFORE = 1
AT = (0, 1, 2, 3)
NT = (((1,), (1,)), ((), ()))
TN = (((0,), (0,)), ((), ()))


def place():
    core = lax.rem(lax.axis_index("island"), 2)
    seq = lax.axis_index("seq")
    x, y = lax.rem(seq, SIDE), seq // SIDE
    a = x + core * (y - x)
    b = y + core * (x - y)
    return a, b, 1 + 3 * core, SIDE - 3 * core


class Wires:
    def __init__(self, send_sems, recv_sems):
        self.send_sems, self.recv_sems, self.count = send_sems, recv_sems, 0

    def send(self, src, dst, device):
        n = self.count
        self.count += 1
        copy = pltpu.make_async_remote_copy(
            src, dst, self.send_sems.at[n], self.recv_sems.at[n], device_id=device, device_id_type=MESH
        )
        copy.start()
        return copy


def span(start, size):
    return pl.ds(pl.multiple_of(start * size, size), size)


def greet(devices):
    barrier = pltpu.get_barrier_semaphore()
    for device in devices:
        pl.semaphore_signal(barrier, inc=1, device_id=device, device_id_type=MESH)
    pl.semaphore_wait(barrier, len(devices))


def weigh(kv, q, do, lse, delta, masks):
    st = lax.dot_general(kv[:, 0:HD], q, NT, preferred_element_type=jnp.float32)
    dpt = lax.dot_general(kv[:, HD : 2 * HD], do, NT, preferred_element_type=jnp.float32)
    probs, dscores = [], []
    for n in range(q.shape[0] // BLK):
        part = slice(n * BLK, (n + 1) * BLK)
        p = jnp.exp2(st[:, part] * (SCALE * LOG2E) - lse[:, part])
        p = jnp.where(masks[n // GROUP], p, 0.0)
        d = p * (dpt[:, part] - delta[:, part])
        probs.append(p.astype(jnp.bfloat16))
        dscores.append(d.astype(jnp.bfloat16))
    return jnp.concatenate(probs, axis=1), jnp.concatenate(dscores, axis=1)


def doc_start(pos, ends):
    begin = jnp.zeros_like(pos)
    for e in ends:
        begin = jnp.where(pos >= e, e, begin)
    return begin


def doc_ends(docs):
    e0 = docs[0]
    e1 = e0 + docs[1]
    return e0, e1, e1 + docs[2]


def gather_kernel(
    order, docs, q_ref, k_ref, v_ref, o_ref, do_ref, lse_ref,
    kv, qs, dos, stats, lkv, ldq,
    o_buf, do_buf, aux, auxx, nq, ndo, nkv, sq, sdo, skv, sstats, sacc, sdq, sj, ssem, rsem, hssem, hrsem, lsem,
):
    a, b, sa, sb = place()
    A = [lax.rem(a + t, SIDE) for t in range(SIDE)]
    B = [lax.rem(b + t, SIDE) for t in range(SIDE)]

    def dev(aa, bb):
        return {"seq": aa * sa + bb * sb}

    def slot(aa, bb):
        return span(aa * sa + bb * sb, ROWS)

    def local(src, dst, n):
        copy = pltpu.make_async_copy(src, dst, lsem.at[n])
        copy.start()
        return copy

    loads = [local(o_ref, o_buf, 0), local(do_ref, do_buf, 1)]
    mine = slot(a, b)
    own_kv = [local(s.at[:, span(a, HD)], kv.at[mine, pl.ds(n * HD, HD)], 2 + n) for n, s in enumerate((k_ref, v_ref))]
    own_q = []
    for h in range(GROUP):
        for n, (s, d) in enumerate(((q_ref, qs), (do_ref, dos))):
            own_q.append(local(s.at[:, span(a * GROUP + h, HD)], d.at[a, h], 4 + 2 * h + n))
    greet([dev(A[1], b), dev(A[3], b), dev(A[2], b), dev(a, B[1]), dev(a, B[3])])
    wires = Wires(ssem, rsem)
    first = {}
    for t in (1, 3, 2):
        first[t] = [
            wires.send(s.at[:, span(A[t], HD)], kv.at[mine, pl.ds(n * HD, HD)], dev(A[t], b))
            for n, s in enumerate((k_ref, v_ref))
        ]
    def head_copy(h, n, t):
        src, dst = ((q_ref, qs), (do_ref, dos))[n]
        sem = (h * 2 + n) * 3 + t - 1
        return pltpu.make_async_remote_copy(
            src.at[:, span(A[t] * GROUP + h, HD)], dst.at[a, h], hssem.at[sem], hrsem.at[sem],
            device_id=dev(A[t], b), device_id_type=MESH,
        )

    def send_head(h):
        for n in range(2):
            for t in (2, 1, 3):
                head_copy(h, n, t).start()

    for h in range(BEFORE):
        send_head(h)

    for load in loads:
        load.wait()
    ones = jnp.ones((8, HD), jnp.bfloat16)
    aux[...] = jnp.zeros_like(aux)
    for g in range(SIDE):
        for h in range(GROUP):
            n = g * GROUP + h
            cols = slice(n * HD, (n + 1) * HD)
            prod = o_buf[:, cols].astype(jnp.float32) * do_buf[:, cols].astype(jnp.float32)
            high = prod.astype(jnp.bfloat16)
            low = (prod - high.astype(jnp.float32)).astype(jnp.bfloat16)
            delta = lax.dot_general(ones, high, NT, preferred_element_type=jnp.float32)
            delta += lax.dot_general(ones, low, NT, preferred_element_type=jnp.float32)
            aux[g, h : h + 1, :] = lse_ref[n : n + 1, :] * LOG2E
            aux[g, 8 + h : 9 + h, :] = delta[0:1]
    facts = [wires.send(aux.at[A[t]], auxx.at[a], dev(A[t], b)) for t in (1, 3, 2)]
    own_q.append(local(aux.at[a], auxx.at[a], 14))
    for h in range(BEFORE, GROUP):
        send_head(h)

    passed = {}

    def spread(t):
        rows = slot(A[t], b)
        passed[t] = (
            wires.send(kv.at[rows], kv.at[rows], dev(a, B[1])),
            wires.send(kv.at[rows], kv.at[rows], dev(a, B[3])),
        )

    for copy in own_kv:
        copy.wait()
    spread(0)
    for t in (1, 3, 2):
        for copy in first[SIDE - t]:
            copy.wait_recv()
        spread(t)
    for copy in own_q + facts:
        copy.wait()
    for m in range(NLOC):
        tok = slice((m % 2) * BLK, (m % 2 + 1) * BLK)
        for h in range(GROUP):
            part = slice(h * BLK, (h + 1) * BLK)
            stats[m, 0:1, part] = auxx[m // 2, h : h + 1, tok]
            stats[m, 1:2, part] = auxx[m // 2, 8 + h : 9 + h, tok]

    ends = doc_ends(docs)
    js = [order[(m // 2 * sa + b * sb) * 2 + m % 2] for m in range(NLOC)]
    ranks = [
        sum((js[i] < js[m] if i > m else js[i] <= js[m]).astype(jnp.int32) for i in range(NLOC) if i != m)
        for m in range(NLOC)
    ]
    for m in range(NLOC):
        nkv[m] = kv[span((m // 2 * sa + b * sb) * 2 + m % 2, BLK), :]
    kinds = [sum(jnp.where(ranks[i] == r, i, 0) for i in range(NLOC)) for r in range(NLOC)]
    for r, m in enumerate(kinds):
        sj[r] = sum(jnp.where(ranks[i] == r, js[i], 0) for i in range(NLOC))
        skv[r * BLK : (r + 1) * BLK, :] = nkv[m]
        facts_r = stats[m]
        for h in range(GROUP):
            sstats[h, :, r * BLK : (r + 1) * BLK] = facts_r[:, h * BLK : (h + 1) * BLK]
    sacc[...] = jnp.zeros_like(sacc)
    iota = lax.broadcasted_iota(jnp.int32, (BLK, BLK), 0)
    kpos = [sj[r] * BLK + iota for r in range(NLOC)]
    qpos = [sj[r] * BLK + lax.broadcasted_iota(jnp.int32, (1, BLK), 1) for r in range(NLOC)]
    qbegin = [doc_start(pos, ends) for pos in qpos]

    second = {}

    def forward(t):
        up, down = passed[t]
        if t in (0, 1):
            up.wait_recv()
            rows = slot(A[t], B[3])
            second[t] = wires.send(kv.at[rows], kv.at[rows], dev(a, B[1]))
        else:
            down.wait_recv()
            rows = slot(A[t], B[1])
            second[t] = wires.send(kv.at[rows], kv.at[rows], dev(a, B[3]))

    def head(h, carry):
        for n in range(2):
            for t in (2, 1, 3):
                head_copy(h, n, t).wait_recv()
        for m in range(NLOC):
            half = slice(m % 2 * BLK, (m % 2 + 1) * BLK)
            nq[m] = qs[m // 2, h, half, :]
            ndo[m] = dos[m // 2, h, half, :]
        for r, m in enumerate(kinds):
            sq[r * BLK : (r + 1) * BLK, :] = nq[m]
            sdo[r * BLK : (r + 1) * BLK, :] = ndo[m]
        st = sstats[h]
        work = []
        for m in range(SIDE):
            keys = skv[0 : (m + 1) * PAIR, :]
            wide = slice(m * PAIR, (m + 1) * PAIR)
            q, do = sq[wide, :], sdo[wide, :]
            sc = lax.dot_general(keys[:, 0:HD], q, NT, preferred_element_type=jnp.float32)
            dp = lax.dot_general(keys[:, HD : 2 * HD], do, NT, preferred_element_type=jnp.float32)
            probs, dscores = [], []
            for u in range(2):
                r = 2 * m + u
                part = slice(u * BLK, (u + 1) * BLK)
                masks = [kpos[n] >= qbegin[r] for n in range(2 * m)]
                masks += [(kpos[n] >= qbegin[r]) & (kpos[n] <= qpos[r]) for n in (2 * m, 2 * m + 1)]
                tok = slice(r * BLK, (r + 1) * BLK)
                p = jnp.exp2(sc[:, part] * (SCALE * LOG2E) - st[0:1, tok])
                p = jnp.where(jnp.concatenate(masks), p, 0.0)
                d = p * (dp[:, part] - st[1:2, tok])
                probs.append(p.astype(jnp.bfloat16))
                dscores.append(d.astype(jnp.bfloat16))
            work.append((keys, q, do, jnp.concatenate(probs, axis=1), jnp.concatenate(dscores, axis=1)))
        for m, (keys, q, do, p, d) in enumerate(work):
            gv = jnp.dot(p, do, preferred_element_type=jnp.float32)
            gk = jnp.dot(d, q, preferred_element_type=jnp.float32)
            for r in range(2 * m + 2):
                rows = slice(r * BLK, (r + 1) * BLK)
                sacc[r, :, HD : 2 * HD] += gv[rows]
                sacc[r, :, 0:HD] += gk[rows]
            g = lax.dot_general(keys[:, 0:HD], d, TN, preferred_element_type=jnp.float32)
            for u in range(2):
                sdq[2 * m + u, h] = g[:, u * BLK : (u + 1) * BLK]
        return carry

    done = 0
    for t, upto in zip((0, 3, 1, 2), AT):
        if upto > done:
            lax.fori_loop(done, upto, head, 0)
            done = upto
        forward(t)
    lax.fori_loop(done, GROUP, head, 0)
    for m in range(NLOC):
        lkv[m] = sacc[ranks[m]]
        ldq[m] = sdq[ranks[m]]

    for t in (0, 1):
        passed[t][1].wait_recv()
    for t in (2, 3):
        passed[t][0].wait_recv()
    for t in range(SIDE):
        second[t].wait()
        for copy in passed[t]:
            copy.wait_send()
    for t in (1, 3, 2):
        for copy in first[t]:
            copy.wait_send()
    for h in range(GROUP):
        for n in range(2):
            for t in (1, 2, 3):
                head_copy(h, n, t).wait_send()


def attend_kernel(order, docs, kv, qs, dos, stats, acc, dqt, inverse, jq, iq, ik):
    a, b, sa, sb = place()
    core = lax.rem(lax.axis_index("island"), 2)
    ends = doc_ends(docs)

    def invert(n, carry):
        inverse[order[n]] = n
        return carry

    lax.fori_loop(0, NBLK, invert, 0, unroll=4)
    acc[...] = jnp.zeros_like(acc)
    dqt[...] = jnp.zeros_like(dqt)

    def plan(i, p):
        j = order[(i // 2 * sa + b * sb) * 2 + lax.rem(i, 2)]
        jq[i] = j
        low = doc_start(j * BLK, ends) // BLK

        def look(c, p):
            seq = inverse[c] // 2
            x, y = lax.rem(seq, SIDE), seq // SIDE
            ik[p] = c
            return p + (y + core * (x - y) != b).astype(jnp.int32)

        q = lax.fori_loop(low, j, look, p)
        ik[q] = -1
        q = q + lax.rem(q, 2)

        def name(t, carry):
            iq[t] = i
            return carry

        lax.fori_loop(p // 2, q // 2, name, 0)
        return q

    total = lax.fori_loop(0, NLOC, plan, 0) // 2
    for u in range(DEEP - 1):
        iq[total + u] = 0
        ik[2 * (total + u)] = -1
        ik[2 * (total + u) + 1] = -1

    def front(t):
        i = iq[t]
        c = [ik[2 * t + u] for u in range(2)]
        at = [span(inverse[jnp.maximum(n, 0)], BLK) for n in c]
        keys = jnp.concatenate([kv[n, :] for n in at])
        q = qs[i // 2, :, span(lax.rem(i, 2), BLK), :].reshape(QW, HD)
        do = dos[i // 2, :, span(lax.rem(i, 2), BLK), :].reshape(QW, HD)
        st = stats[i]
        pos = jq[i] * BLK + lax.broadcasted_iota(jnp.int32, (1, BLK), 1)
        iota = lax.broadcasted_iota(jnp.int32, (BLK, BLK), 0)
        kpos = jnp.concatenate([n * BLK + iota for n in c])
        mask = (kpos >= doc_start(pos, ends)) & (kpos <= pos)
        p, d = weigh(keys, q, do, st[0:1], st[1:2], [mask])
        return i, at, keys, q, do, p, d

    def back(i, at, keys, q, do, p, d):
        gv = jnp.dot(p, do, preferred_element_type=jnp.float32)
        gk = jnp.dot(d, q, preferred_element_type=jnp.float32)
        for n in range(2):
            acc[at[n], HD : 2 * HD] += gv[n * BLK : (n + 1) * BLK]
            acc[at[n], 0:HD] += gk[n * BLK : (n + 1) * BLK]
        dqt[i] += lax.dot_general(keys[:, 0:HD], d, TN, preferred_element_type=jnp.float32)

    def step(s, carry):
        work = [front(s * DEEP + u) for u in range(DEEP)]
        for item in work:
            back(*item)
        return carry

    lax.fori_loop(0, (total + DEEP - 1) // DEEP, step, 0)


def scatter_kernel(
    acc, dqt, lkv, ldq, dq, dk, dv, sent, mid, thr, got, grads, dqs, ssem, rsem, lsem
):
    a, b, sa, sb = place()
    A = [lax.rem(a + t, SIDE) for t in range(SIDE)]
    B = [lax.rem(b + t, SIDE) for t in range(SIDE)]

    def dev(aa, bb):
        return {"seq": aa * sa + bb * sb}

    def slot(aa, bb):
        return span(aa * sa + bb * sb, ROWS)

    up, down = dev(a, B[1]), dev(a, B[3])
    toward = (up, up, down, down)
    next_b = (B[1], B[1], B[3], B[3])
    other_b = (B[3], B[3], B[1], B[1])
    other = (down, down, up, up)
    for t in range(SIDE):
        sent[t] = acc[slot(A[t], B[2]), :].astype(jnp.bfloat16)
    greet([dev(A[1], b), dev(A[3], b), dev(A[2], b), up, down])
    wires = Wires(ssem, rsem)
    through = [wires.send(sent.at[t], thr.at[t], toward[t]) for t in range(SIDE)]
    plain = [None] * SIDE
    for t in (0, 2, 1, 3):
        sent[SIDE + t] = acc[slot(A[t], other_b[t]), :].astype(jnp.bfloat16)
        plain[t] = wires.send(sent.at[SIDE + t], got.at[1 if t < 2 else 0, t], other[t])

    def finish(t):
        for u in range(2):
            m = 2 * A[t] + u
            for h in range(GROUP):
                part = slice(h * BLK, (h + 1) * BLK)
                g = (dqt[m, :, part] + ldq[m, h]) * SCALE
                dqs[t, u * BLK : (u + 1) * BLK, part] = g.T.astype(jnp.bfloat16)

    heads = []
    for t in (2, 1, 3):
        finish(t)
        heads.append(wires.send(dqs.at[t], dq.at[:, span(a, QW)], dev(A[t], b)))
    summed = [None] * SIDE
    for t in (0, 2, 1, 3):
        through[t].wait_recv()
        total = acc[slot(A[t], next_b[t]), :] + thr[t].astype(jnp.float32)
        mid[t] = total.astype(jnp.bfloat16)
        summed[t] = wires.send(mid.at[t], got.at[0 if t < 2 else 1, t], toward[t])
    finish(0)
    copies = [pltpu.make_async_copy(dqs.at[0], dq.at[:, span(a, QW)], lsem.at[0])]
    copies[0].start()
    last = []
    for t in (2, 1, 3, 0):
        plain[t].wait_recv()
        summed[t].wait_recv()
        own = lkv[pl.ds(2 * A[t], 2)].reshape(ROWS, 2 * HD)
        total = own + got[0, t].astype(jnp.float32) + got[1, t].astype(jnp.float32)
        grads[t, :, 0:HD] = (total[:, 0:HD] * SCALE).astype(jnp.bfloat16)
        grads[t, :, HD : 2 * HD] = total[:, HD : 2 * HD].astype(jnp.bfloat16)
        for n, d in enumerate((dk, dv)):
            src = grads.at[t, :, pl.ds(n * HD, HD)]
            if t:
                last.append(wires.send(src, d.at[:, span(a, HD)], dev(A[t], b)))
            else:
                copy = pltpu.make_async_copy(src, d.at[:, span(a, HD)], lsem.at[1 + n])
                copy.start()
                copies.append(copy)
    for copy in heads + last:
        copy.wait()
    for copy in through + plain + summed:
        copy.wait_send()
    for copy in copies:
        copy.wait()


ANY = pl.BlockSpec(memory_space=pl.ANY)
HBM = pl.BlockSpec(memory_space=pltpu.HBM)
VMEM = pl.BlockSpec(memory_space=pltpu.VMEM)
SMEM = pl.BlockSpec(memory_space=pltpu.SMEM)
BF = jnp.bfloat16
F32 = jnp.float32
MIB = 2**20


def shapes(*pairs):
    return [jax.ShapeDtypeStruct(s, d) for s, d in pairs]


def gather_call(order, docs, query, key, value, attn_out, out_grad, log_sums):
    packed = (SIDE, GROUP, ROWS, HD)
    return pl.pallas_call(
        gather_kernel,
        out_shape=shapes(
            ((TOKENS, 2 * HD), BF), (packed, BF), (packed, BF), ((NLOC, 8, QW), F32),
            ((NLOC, BLK, 2 * HD), F32), ((NLOC, GROUP, HD, BLK), F32),
        ),
        in_specs=[SMEM, SMEM] + [HBM] * 5 + [VMEM],
        out_specs=[VMEM] * 6,
        scratch_shapes=[
            pltpu.VMEM((ROWS, SIDE * QW), BF),
            pltpu.VMEM((ROWS, SIDE * QW), BF),
            pltpu.VMEM((SIDE, 16, ROWS), F32),
            pltpu.VMEM((SIDE, 16, ROWS), F32),
            pltpu.VMEM((NLOC, BLK, HD), BF),
            pltpu.VMEM((NLOC, BLK, HD), BF),
            pltpu.VMEM((NLOC, BLK, 2 * HD), BF),
            pltpu.VMEM((NLOC * BLK, HD), BF),
            pltpu.VMEM((NLOC * BLK, HD), BF),
            pltpu.VMEM((NLOC * BLK, 2 * HD), BF),
            pltpu.VMEM((GROUP, 8, NLOC * BLK), F32),
            pltpu.VMEM((NLOC, BLK, 2 * HD), F32),
            pltpu.VMEM((NLOC, GROUP, HD, BLK), F32),
            pltpu.SMEM((NLOC,), jnp.int32),
            pltpu.SemaphoreType.DMA((24,)),
            pltpu.SemaphoreType.DMA((24,)),
            pltpu.SemaphoreType.DMA((30,)),
            pltpu.SemaphoreType.DMA((30,)),
            pltpu.SemaphoreType.DMA((16,)),
        ],
        compiler_params=pltpu.CompilerParams(
            collective_id=1, has_side_effects=True, vmem_limit_bytes=49 * MIB
        ),
        name="gather",
    )(order, docs, query, key, value, attn_out, out_grad, log_sums)


def attend_call(order, docs, kv, qs, dos, stats):
    return pl.pallas_call(
        attend_kernel,
        out_shape=shapes(((TOKENS, 2 * HD), F32), ((NLOC, HD, QW), F32)),
        in_specs=[SMEM, SMEM] + [VMEM] * 4,
        out_specs=[VMEM, VMEM],
        scratch_shapes=[
            pltpu.SMEM((NBLK,), jnp.int32),
            pltpu.SMEM((NLOC,), jnp.int32),
            pltpu.SMEM((128,), jnp.int32),
            pltpu.SMEM((256,), jnp.int32),
        ],
        compiler_params=pltpu.CompilerParams(vmem_limit_bytes=28 * MIB),
        name="attend",
    )(order, docs, kv, qs, dos, stats)


def scatter_call(acc, dqt, lkv, ldq):
    piece = (SIDE, ROWS, 2 * HD)
    return pl.pallas_call(
        scatter_kernel,
        out_shape=shapes(((ROWS, SIDE * QW), BF), ((ROWS, SIDE * HD), BF), ((ROWS, SIDE * HD), BF)),
        in_specs=[VMEM] * 4,
        out_specs=[ANY] * 3,
        scratch_shapes=[
            pltpu.VMEM((2 * SIDE, ROWS, 2 * HD), BF),
            pltpu.VMEM(piece, BF),
            pltpu.VMEM(piece, BF),
            pltpu.VMEM((2,) + piece, BF),
            pltpu.VMEM(piece, BF),
            pltpu.VMEM((SIDE, ROWS, QW), BF),
            pltpu.SemaphoreType.DMA((24,)),
            pltpu.SemaphoreType.DMA((24,)),
            pltpu.SemaphoreType.DMA((4,)),
        ],
        compiler_params=pltpu.CompilerParams(
            collective_id=2, has_side_effects=True, vmem_limit_bytes=28 * MIB
        ),
        name="scatter",
    )(acc, dqt, lkv, ldq)


def body(query, key, value, attn_out, out_grad, log_sums, block_order, doc_lengths):
    kv, qs, dos, stats, lkv, ldq = gather_call(
        block_order, doc_lengths, query, key, value, attn_out, out_grad, log_sums
    )
    acc, dqt = attend_call(block_order, doc_lengths, kv, qs, dos, stats)
    return scatter_call(acc, dqt, lkv, ldq)


def solution(mesh):
    rows = P(("island", "seq"), None)
    return jax.shard_map(
        body,
        mesh=mesh,
        in_specs=(rows,) * 5 + (P(None, ("island", "seq")), P("island"), P("island")),
        out_specs=(rows,) * 3,
        check_vma=False,
    )
```

time: 98.8 us -> 90.9 us (0.920)
  the two profiles are of different devices: /device:TPU:0 before, /device:TPU:1 now
where the time goes in v2:
time: 90.9 us; the launch traced here: 90.7 us
  Pallas kernels  82 us (90%)
  local copies, waits for them, and re-layouts  7.99 us (9%)
    pallas_call x1, Pallas kernels, gather_call(): pl.pallas_call(gather_kernel, out_shape=shapes(((TOKENS, 2 * HD), BF), (p...  38.3 us
    pallas_call x1, Pallas kernels, scatter_call(): pl.pallas_call(scatter_kernel, out_shape=shapes(((ROWS, SIDE * QW), BF),...  23.9 us
    pallas_call x1, Pallas kernels, attend_call(): pl.pallas_call(attend_kernel, out_shape=shapes(((TOKENS, 2 * HD), F32), (...  19.7 us
    unnamed x17, local copies, waits for them, and re-layouts  7.99 us

profile of v2, /device:TPU:1, one launch (start us, length us, event | category | flops | bytes accessed | tf_op | source)
XLA Modules:
  0.0 90.7 jit_solution(7151301949801388332)
XLA Ops:
  0.6 0.0 copy-start.2
  0.6 0.9 %copy-done.2 = bf16[256,512]{1,0:T(8,128)(2,1)S(1)} copy-done((bf16[256,512]{1,0:T(8,128)(2,1)S(1)}, bf16[256,512]{1,0:T(8,128)(2,1)}, u32[]{:S(2)}) %copy-start.2) | copy-done | bytes 262168
  1.6 0.0 copy-start.3
  1.6 0.9 %copy-done.3 = bf16[256,512]{1,0:T(8,128)(2,1)S(1)} copy-done((bf16[256,512]{1,0:T(8,128)(2,1)S(1)}, bf16[256,512]{1,0:T(8,128)(2,1)}, u32[]{:S(2)}) %copy-start.3) | copy-done | bytes 262168
  2.5 0.0 copy-start.4
  2.5 0.7 copy-done.4
  3.3 0.0 copy-start.5
  3.3 0.7 copy-done.5
  3.9 0.0 copy-start.6
  3.9 0.7 copy-done.6
  4.6 38.3 %gather.1 = (bf16[4096,256]{1,0:T(8,128)(2,1)}, bf16[4,5,256,128]{3,2,1,0:T(8,128)(2,1)S(1)}, bf16[4,5,256,128]{3,2,1,0:T(8,128)(2,1)S(1)}, f32[8,8,640]{2,1,0:T...) custom-call(s32[32]{0:T(128)S(1)} %copy-done.5, s32[4]{0:T(128)S(1)} %copy-done.6, ...), custom_call_target="tpu_custom_call" | custom-call | tf_op jit(solution)/shard_map/gather/pallas_call | solution.py:455
  42.9 0.0 copy-start.1
  42.9 1.6 %copy-done.1 = bf16[4096,256]{1,0:T(8,128)(2,1)S(1)} copy-done((bf16[4096,256]{1,0:T(8,128)(2,1)S(1)}, bf16[4096,256]{1,0:T(8,128)(2,1)}, u32[]{:S(2)}) %copy-start.1) | copy-done | bytes 2097176
  44.5 0.0 copy-start
  44.5 19.7 %attend.1 = (f32[4096,256]{1,0:T(8,128)S(1)}, f32[8,128,640]{2,1,0:T(8,128)S(1)}) custom-call(s32[32]{0:T(128)S(1)} %copy-done.5, s32[4]{0:T(128)S(1)} %copy-done.6, bf16[4096,256]{1,0:T(8,128)(2,1)S(1)} %copy-done.1, bf16[4,5,256,128]{3,2,1,0:T(8,128)(2,1)S(1)} %get-tuple-element.12.qs, bf16[4,5,256,128]{3,2,1,0:T(8,128)(2,1)S(1)} %get-tuple-element.13.dos, ...), custom_call_target="tpu_custom_call" | custom-call | tf_op jit(solution)/shard_map/attend/pallas_call | solution.py:492
  64.2 0.0 copy-done
  64.2 23.9 %scatter.1 = (bf16[256,2560]{1,0:T(8,128)(2,1)S(1)}, bf16[256,512]{1,0:T(8,128)(2,1)S(1)}, bf16[256,512]{1,0:T(8,128)(2,1)S(1)}) custom-call(f32[4096,256]{1,0:T(8,128)S(1)} %get-tuple-element.15.acc, f32[8,128,640]{2,1,0:T(8,128)S(1)} %get-tuple-element.16.dqt, f32[8,128,256]{2,1,0:T(8,128)S(1)} %get-tuple-element.17.lkv, f32[8,5,128,128]{3,2,1,0:T(8,128)S(1)} %copy-done), custom_call_target="tpu_custom_call" | custom-call | tf_op jit(solution)/shard_map/scatter/pallas_call | solution.py:510
  88.2 1.1 %copy.14 = bf16[256,2560]{1,0:T(8,128)(2,1)} copy(bf16[256,2560]{1,0:T(8,128)(2,1)S(1)} %get-tuple-element.22) | data formatting | bytes 2621440
  89.3 0.7 copy.15
  90.0 0.7 copy.16
Async XLA Ops:
  0.6 1.0 %copy-start.2 = (bf16[256,512]{1,0:T(8,128)(2,1)S(1)}, bf16[256,512]{1,0:T(8,128)(2,1)}, u32[]{:S(2)}) copy-start(bf16[256,512]{1,0:T(8,128)(2,1)} %k_ref.1) | copy-start | bytes 786436
  1.6 0.9 %copy-start.3 = (bf16[256,512]{1,0:T(8,128)(2,1)S(1)}, bf16[256,512]{1,0:T(8,128)(2,1)}, u32[]{:S(2)}) copy-start(bf16[256,512]{1,0:T(8,128)(2,1)} %v_ref.1) | copy-start | bytes 786436
  2.5 0.7 copy-start.4
  3.3 0.7 copy-start.5
  3.9 0.7 copy-start.6
  42.9 1.6 %copy-start.1 = (bf16[4096,256]{1,0:T(8,128)(2,1)S(1)}, bf16[4096,256]{1,0:T(8,128)(2,1)}, u32[]{:S(2)}) copy-start(bf16[4096,256]{1,0:T(8,128)(2,1)} %get-tuple-element.11.kv) | copy-start | bytes 6291460
  44.5 19.8 %copy-start = (f32[8,5,128,128]{3,2,1,0:T(8,128)S(1)}, f32[8,5,128,128]{3,2,1,0:T(8,128)}, u32[]{:S(2)}) copy-start(f32[8,5,128,128]{3,2,1,0:T(8,128)} %get-tuple-element.18.ldq) | copy-start | bytes 7864324

commit v3 on v2

--- a/solution.py
+++ b/solution.py
@@ -21,9 +21,9 @@
 NLOC = 2 * SIDE
 SCALE = 1.0 / math.sqrt(HD)
 LOG2E = math.log2(math.e)
-DEEP = 2
+DEEP = 4
 BEFORE = 1
-AT = (0, 1, 2, 3)
+AT = (1, 2, 3, 4)
 NT = (((1,), (1,)), ((), ()))
 TN = (((0,), (0,)), ((), ()))
 
@@ -62,14 +62,14 @@
     pl.semaphore_wait(barrier, len(devices))
 
 
-def weigh(kv, q, do, lse, delta, masks):
-    st = lax.dot_general(kv[:, 0:HD], q, NT, preferred_element_type=jnp.float32)
-    dpt = lax.dot_general(kv[:, HD : 2 * HD], do, NT, preferred_element_type=jnp.float32)
+def weigh(keys, values, q, do, lse, delta, mask):
+    st = lax.dot_general(keys, q, NT, preferred_element_type=jnp.float32)
+    dpt = lax.dot_general(values, do, NT, preferred_element_type=jnp.float32)
     probs, dscores = [], []
     for n in range(q.shape[0] // BLK):
         part = slice(n * BLK, (n + 1) * BLK)
         p = jnp.exp2(st[:, part] * (SCALE * LOG2E) - lse[:, part])
-        p = jnp.where(masks[n // GROUP], p, 0.0)
+        p = jnp.where(mask, p, 0.0)
         d = p * (dpt[:, part] - delta[:, part])
         probs.append(p.astype(jnp.bfloat16))
         dscores.append(d.astype(jnp.bfloat16))
@@ -83,15 +83,15 @@
     return begin
 
 
-def doc_ends(docs):
-    e0 = docs[0]
-    e1 = e0 + docs[1]
-    return e0, e1, e1 + docs[2]
+def doc_ends(facts):
+    e0 = facts[NBLK]
+    e1 = e0 + facts[NBLK + 1]
+    return e0, e1, e1 + facts[NBLK + 2]
 
 
 def gather_kernel(
-    order, docs, q_ref, k_ref, v_ref, o_ref, do_ref, lse_ref,
-    kv, qs, dos, stats, lkv, ldq,
+    facts_ref, q_ref, kv_ref, o_ref, do_ref, lse_ref,
+    ks, vs, qs, dos, stats, lkv, l0, l1, l2, l3, l4,
     o_buf, do_buf, aux, auxx, nq, ndo, nkv, sq, sdo, skv, sstats, sacc, sdq, sj, ssem, rsem, hssem, hrsem, lsem,
 ):
     a, b, sa, sb = place()
@@ -104,6 +104,9 @@
     def slot(aa, bb):
         return span(aa * sa + bb * sb, ROWS)
 
+    kvs = (ks, vs)
+    ldq = (l0, l1, l2, l3, l4)
+
     def local(src, dst, n):
         copy = pltpu.make_async_copy(src, dst, lsem.at[n])
         copy.start()
@@ -111,7 +114,7 @@
 
     loads = [local(o_ref, o_buf, 0), local(do_ref, do_buf, 1)]
     mine = slot(a, b)
-    own_kv = [local(s.at[:, span(a, HD)], kv.at[mine, pl.ds(n * HD, HD)], 2 + n) for n, s in enumerate((k_ref, v_ref))]
+    own_kv = [local(kv_ref.at[:, span(a + SIDE * n, HD)], kvs[n].at[mine], 2 + n) for n in range(2)]
     own_q = []
     for h in range(GROUP):
         for n, (s, d) in enumerate(((q_ref, qs), (do_ref, dos))):
@@ -121,8 +124,8 @@
     first = {}
     for t in (1, 3, 2):
         first[t] = [
-            wires.send(s.at[:, span(A[t], HD)], kv.at[mine, pl.ds(n * HD, HD)], dev(A[t], b))
-            for n, s in enumerate((k_ref, v_ref))
+            wires.send(kv_ref.at[:, span(A[t] + SIDE * n, HD)], kvs[n].at[mine], dev(A[t], b))
+            for n in range(2)
         ]
     def head_copy(h, n, t):
         src, dst = ((q_ref, qs), (do_ref, dos))[n]
@@ -164,10 +167,7 @@
 
     def spread(t):
         rows = slot(A[t], b)
-        passed[t] = (
-            wires.send(kv.at[rows], kv.at[rows], dev(a, B[1])),
-            wires.send(kv.at[rows], kv.at[rows], dev(a, B[3])),
-        )
+        passed[t] = [[wires.send(x.at[rows], x.at[rows], dev(a, B[n])) for x in kvs] for n in (1, 3)]
 
     for copy in own_kv:
         copy.wait()
@@ -185,14 +185,16 @@
             stats[m, 0:1, part] = auxx[m // 2, h : h + 1, tok]
             stats[m, 1:2, part] = auxx[m // 2, 8 + h : 9 + h, tok]
 
-    ends = doc_ends(docs)
+    order = facts_ref
+    ends = doc_ends(order)
     js = [order[(m // 2 * sa + b * sb) * 2 + m % 2] for m in range(NLOC)]
     ranks = [
         sum((js[i] < js[m] if i > m else js[i] <= js[m]).astype(jnp.int32) for i in range(NLOC) if i != m)
         for m in range(NLOC)
     ]
     for m in range(NLOC):
-        nkv[m] = kv[span((m // 2 * sa + b * sb) * 2 + m % 2, BLK), :]
+        here = span((m // 2 * sa + b * sb) * 2 + m % 2, BLK)
+        nkv[m] = jnp.concatenate([ks[here, :], vs[here, :]], axis=1)
     kinds = [sum(jnp.where(ranks[i] == r, i, 0) for i in range(NLOC)) for r in range(NLOC)]
     for r, m in enumerate(kinds):
         sj[r] = sum(jnp.where(ranks[i] == r, js[i], 0) for i in range(NLOC))
@@ -210,14 +212,10 @@
 
     def forward(t):
         up, down = passed[t]
-        if t in (0, 1):
-            up.wait_recv()
-            rows = slot(A[t], B[3])
-            second[t] = wires.send(kv.at[rows], kv.at[rows], dev(a, B[1]))
-        else:
-            down.wait_recv()
-            rows = slot(A[t], B[1])
-            second[t] = wires.send(kv.at[rows], kv.at[rows], dev(a, B[3]))
+        for copy in up if t < 2 else down:
+            copy.wait_recv()
+        rows = slot(A[t], B[3] if t < 2 else B[1])
+        second[t] = [wires.send(x.at[rows], x.at[rows], dev(a, B[1] if t < 2 else B[3])) for x in kvs]
 
     def head(h, carry):
         for n in range(2):
@@ -272,15 +270,16 @@
     lax.fori_loop(done, GROUP, head, 0)
     for m in range(NLOC):
         lkv[m] = sacc[ranks[m]]
-        ldq[m] = sdq[ranks[m]]
-
-    for t in (0, 1):
-        passed[t][1].wait_recv()
-    for t in (2, 3):
-        passed[t][0].wait_recv()
+        mine_dq = sdq[ranks[m]]
+        for h in range(GROUP):
+            ldq[h][m] = mine_dq[h]
+
     for t in range(SIDE):
-        second[t].wait()
-        for copy in passed[t]:
+        for copy in passed[t][1 if t < 2 else 0]:
+            copy.wait_recv()
+        for copy in second[t]:
+            copy.wait()
+        for copy in passed[t][0] + passed[t][1]:
             copy.wait_send()
     for t in (1, 3, 2):
         for copy in first[t]:
@@ -291,10 +290,10 @@
                 head_copy(h, n, t).wait_send()
 
 
-def attend_kernel(order, docs, kv, qs, dos, stats, acc, dqt, inverse, jq, iq, ik):
+def attend_kernel(order, ks, vs, qs, dos, stats, acc, dqt, inverse, jq, iq, ik):
     a, b, sa, sb = place()
     core = lax.rem(lax.axis_index("island"), 2)
-    ends = doc_ends(docs)
+    ends = doc_ends(order)
 
     def invert(n, carry):
         inverse[order[n]] = n
@@ -327,16 +326,12 @@
         return q
 
     total = lax.fori_loop(0, NLOC, plan, 0) // 2
-    for u in range(DEEP - 1):
-        iq[total + u] = 0
-        ik[2 * (total + u)] = -1
-        ik[2 * (total + u) + 1] = -1
-
     def front(t):
         i = iq[t]
         c = [ik[2 * t + u] for u in range(2)]
         at = [span(inverse[jnp.maximum(n, 0)], BLK) for n in c]
-        keys = jnp.concatenate([kv[n, :] for n in at])
+        keys = jnp.concatenate([ks[n, :] for n in at])
+        values = jnp.concatenate([vs[n, :] for n in at])
         q = qs[i // 2, :, span(lax.rem(i, 2), BLK), :].reshape(QW, HD)
         do = dos[i // 2, :, span(lax.rem(i, 2), BLK), :].reshape(QW, HD)
         st = stats[i]
@@ -344,7 +339,7 @@
         iota = lax.broadcasted_iota(jnp.int32, (BLK, BLK), 0)
         kpos = jnp.concatenate([n * BLK + iota for n in c])
         mask = (kpos >= doc_start(pos, ends)) & (kpos <= pos)
-        p, d = weigh(keys, q, do, st[0:1], st[1:2], [mask])
+        p, d = weigh(keys, values, q, do, st[0:1], st[1:2], mask)
         return i, at, keys, q, do, p, d
 
     def back(i, at, keys, q, do, p, d):
@@ -353,19 +348,30 @@
         for n in range(2):
             acc[at[n], HD : 2 * HD] += gv[n * BLK : (n + 1) * BLK]
             acc[at[n], 0:HD] += gk[n * BLK : (n + 1) * BLK]
-        dqt[i] += lax.dot_general(keys[:, 0:HD], d, TN, preferred_element_type=jnp.float32)
+        dqt[i] += lax.dot_general(keys, d, TN, preferred_element_type=jnp.float32)
+
+    def group(first, size):
+        held = front(first)
+        for u in range(1, size):
+            following = front(first + u)
+            back(*held)
+            held = following
+        back(*held)
 
     def step(s, carry):
-        work = [front(s * DEEP + u) for u in range(DEEP)]
-        for item in work:
-            back(*item)
+        group(s * DEEP, DEEP)
         return carry
 
-    lax.fori_loop(0, (total + DEEP - 1) // DEEP, step, 0)
+    def single(s, carry):
+        group(s, 1)
+        return carry
+
+    lax.fori_loop(0, total // DEEP, step, 0)
+    lax.fori_loop(total // DEEP * DEEP, total, single, 0)
 
 
 def scatter_kernel(
-    acc, dqt, lkv, ldq, dq, dk, dv, sent, mid, thr, got, grads, dqs, ssem, rsem, lsem
+    acc, dqt, lkv, l0, l1, l2, l3, l4, dq, dk, dv, sent, mid, thr, got, grads, dqs, ssem, rsem, lsem
 ):
     a, b, sa, sb = place()
     A = [lax.rem(a + t, SIDE) for t in range(SIDE)]
@@ -397,7 +403,7 @@
             m = 2 * A[t] + u
             for h in range(GROUP):
                 part = slice(h * BLK, (h + 1) * BLK)
-                g = (dqt[m, :, part] + ldq[m, h]) * SCALE
+                g = (dqt[m, :, part] + (l0, l1, l2, l3, l4)[h][m]) * SCALE
                 dqs[t, u * BLK : (u + 1) * BLK, part] = g.T.astype(jnp.bfloat16)
 
     heads = []
@@ -437,6 +443,15 @@
         copy.wait()
 
 
+def emit_kernel(*refs):
+    sems = refs[-1]
+    copies = [pltpu.make_async_copy(refs[n], refs[n + 3], sems.at[n]) for n in range(3)]
+    for copy in copies:
+        copy.start()
+    for copy in copies:
+        copy.wait()
+
+
 ANY = pl.BlockSpec(memory_space=pl.ANY)
 HBM = pl.BlockSpec(memory_space=pltpu.HBM)
 VMEM = pl.BlockSpec(memory_space=pltpu.VMEM)
@@ -450,16 +465,16 @@
     return [jax.ShapeDtypeStruct(s, d) for s, d in pairs]
 
 
-def gather_call(order, docs, query, key, value, attn_out, out_grad, log_sums):
+def gather_call(facts, query, kv, attn_out, out_grad, log_sums):
     packed = (SIDE, GROUP, ROWS, HD)
     return pl.pallas_call(
         gather_kernel,
         out_shape=shapes(
-            ((TOKENS, 2 * HD), BF), (packed, BF), (packed, BF), ((NLOC, 8, QW), F32),
-            ((NLOC, BLK, 2 * HD), F32), ((NLOC, GROUP, HD, BLK), F32),
+            ((TOKENS, HD), BF), ((TOKENS, HD), BF), (packed, BF), (packed, BF), ((NLOC, 8, QW), F32),
+            ((NLOC, BLK, 2 * HD), F32), *[((NLOC, HD, BLK), F32)] * GROUP,
         ),
-        in_specs=[SMEM, SMEM] + [HBM] * 5 + [VMEM],
-        out_specs=[VMEM] * 6,
+        in_specs=[SMEM] + [HBM] * 4 + [VMEM],
+        out_specs=[VMEM] * 11,
         scratch_shapes=[
             pltpu.VMEM((ROWS, SIDE * QW), BF),
             pltpu.VMEM((ROWS, SIDE * QW), BF),
@@ -475,24 +490,24 @@
             pltpu.VMEM((NLOC, BLK, 2 * HD), F32),
             pltpu.VMEM((NLOC, GROUP, HD, BLK), F32),
             pltpu.SMEM((NLOC,), jnp.int32),
-            pltpu.SemaphoreType.DMA((24,)),
-            pltpu.SemaphoreType.DMA((24,)),
+            pltpu.SemaphoreType.DMA((40,)),
+            pltpu.SemaphoreType.DMA((40,)),
             pltpu.SemaphoreType.DMA((30,)),
             pltpu.SemaphoreType.DMA((30,)),
             pltpu.SemaphoreType.DMA((16,)),
         ],
         compiler_params=pltpu.CompilerParams(
-            collective_id=1, has_side_effects=True, vmem_limit_bytes=49 * MIB
+            collective_id=1, has_side_effects=True, vmem_limit_bytes=45 * MIB
         ),
         name="gather",
-    )(order, docs, query, key, value, attn_out, out_grad, log_sums)
-
-
-def attend_call(order, docs, kv, qs, dos, stats):
+    )(facts, query, kv, attn_out, out_grad, log_sums)
+
+
+def attend_call(facts, ks, vs, qs, dos, stats):
     return pl.pallas_call(
         attend_kernel,
         out_shape=shapes(((TOKENS, 2 * HD), F32), ((NLOC, HD, QW), F32)),
-        in_specs=[SMEM, SMEM] + [VMEM] * 4,
+        in_specs=[SMEM] + [VMEM] * 5,
         out_specs=[VMEM, VMEM],
         scratch_shapes=[
             pltpu.SMEM((NBLK,), jnp.int32),
@@ -502,15 +517,15 @@
         ],
         compiler_params=pltpu.CompilerParams(vmem_limit_bytes=28 * MIB),
         name="attend",
-    )(order, docs, kv, qs, dos, stats)
-
-
-def scatter_call(acc, dqt, lkv, ldq):
+    )(facts, ks, vs, qs, dos, stats)
+
+
+def scatter_call(acc, dqt, lkv, *ldq):
     piece = (SIDE, ROWS, 2 * HD)
     return pl.pallas_call(
         scatter_kernel,
         out_shape=shapes(((ROWS, SIDE * QW), BF), ((ROWS, SIDE * HD), BF), ((ROWS, SIDE * HD), BF)),
-        in_specs=[VMEM] * 4,
+        in_specs=[VMEM] * 8,
         out_specs=[ANY] * 3,
         scratch_shapes=[
             pltpu.VMEM((2 * SIDE, ROWS, 2 * HD), BF),
@@ -527,15 +542,27 @@
             collective_id=2, has_side_effects=True, vmem_limit_bytes=28 * MIB
         ),
         name="scatter",
-    )(acc, dqt, lkv, ldq)
+    )(acc, dqt, lkv, *ldq)
+
+
+def emit_call(*grads):
+    return pl.pallas_call(
+        emit_kernel,
+        out_shape=shapes(*((g.shape, g.dtype) for g in grads)),
+        in_specs=[VMEM] * 3,
+        out_specs=[HBM] * 3,
+        scratch_shapes=[pltpu.SemaphoreType.DMA((3,))],
+        compiler_params=pltpu.CompilerParams(vmem_limit_bytes=4 * MIB),
+        name="emit",
+    )(*grads)
 
 
 def body(query, key, value, attn_out, out_grad, log_sums, block_order, doc_lengths):
-    kv, qs, dos, stats, lkv, ldq = gather_call(
-        block_order, doc_lengths, query, key, value, attn_out, out_grad, log_sums
-    )
-    acc, dqt = attend_call(block_order, doc_lengths, kv, qs, dos, stats)
-    return scatter_call(acc, dqt, lkv, ldq)
+    facts = jnp.concatenate([block_order, doc_lengths])
+    kv = jnp.concatenate([key, value], axis=1)
+    ks, vs, qs, dos, stats, lkv, *ldq = gather_call(facts, query, kv, attn_out, out_grad, log_sums)
+    acc, dqt = attend_call(facts, ks, vs, qs, dos, stats)
+    return emit_call(*scatter_call(acc, dqt, lkv, *ldq))
 
 
 def solution(mesh):

time: 90.9 us -> 84.4 us (0.928)
  the two profiles are of different devices: /device:TPU:1 before, /device:TPU:98 now
where the time goes in v3:
time: 84.4 us; the launch traced here: 84.2 us
  Pallas kernels  80.8 us (96%)
  other arithmetic  1.82 us (2%)
    pallas_call x1, Pallas kernels, gather_call(): pl.pallas_call(gather_kernel, out_shape=shapes(((TOKENS, HD), BF), ((TOKE...  35.4 us
    pallas_call x1, Pallas kernels, scatter_call(): pl.pallas_call(scatter_kernel, out_shape=shapes(((ROWS, SIDE * QW), BF),...  33.8 us
    pallas_call x1, Pallas kernels, attend_call(): pl.pallas_call(attend_kernel, out_shape=shapes(((TOKENS, 2 * HD), F32), (...  10.4 us

profile of v3, /device:TPU:98, one launch (start us, length us, event | category | flops | bytes accessed | tf_op | source)
XLA Modules:
  0.0 84.2 jit_solution(17558428316899453388)
XLA Ops:
  0.6 0.7 pad_add_fusion.facts_ref.order
  1.4 1.1 %pad_maximum_fusion.kv_ref = bf16[256,1024]{1,0:T(8,128)(2,1)S(1)} fusion(bf16[256,512]{1,0:T(8,128)(2,1)} %param.10, bf16[256,512]{1,0:T(8,128)(2,1)} %param.9), kind=kLoop, calls=%fused_computation | loop fusion | flops 1048576 | bytes 1048576 | tf_op jit(solution)/shard_map/concatenate | solution.py:562
  2.5 0.0 copy-start
  2.5 0.7 copy-done
  3.2 35.4 %gather.1 = (bf16[4096,128]{1,0:T(8,128)(2,1)S(1)}, bf16[4096,128]{1,0:T(8,128)(2,1)S(1)}, bf16[4,5,256,128]{3,2,1,0:T(8,128)(2,1)S(1)}, bf16[4,5,256,128]{3,2,1...) custom-call(s32[36]{0:T(128)S(1)} %pad_add_fusion.facts_ref.order, ...), custom_call_target="tpu_custom_call" | custom-call | tf_op jit(solution)/shard_map/gather/pallas_call | solution.py:470
  38.6 10.4 %attend.1 = (f32[4096,256]{1,0:T(8,128)S(1)}, f32[8,128,640]{2,1,0:T(8,128)S(1)}) custom-call(s32[36]{0:T(128)S(1)} %pad_add_fusion.facts_ref.order, bf16[4096,128]{1,0:T(8,128)(2,1)S(1)} %get-tuple-element.19.ks, bf16[4096,128]{1,0:T(8,128)(2,1)S(1)} %get-tuple-element.20.vs, bf16[4,5,256,128]{3,2,1,0:T(8,128)(2,1)S(1)} %get-tuple-element.21.qs, ...), custom_call_target="tpu_custom_call" | custom-call | tf_op jit(solution)/shard_map/attend/pallas_call | solution.py:507
  49.0 33.8 %scatter.1 = (bf16[256,2560]{1,0:T(8,128)(2,1)S(1)}, bf16[256,512]{1,0:T(8,128)(2,1)S(1)}, bf16[256,512]{1,0:T(8,128)(2,1)S(1)}) custom-call(f32[4096,256]{1,0:T(8,128)S(1)} %get-tuple-element.24.acc, f32[8,128,640]{2,1,0:T(8,128)S(1)} %get-tuple-element.25.dqt, f32[8,128,256]{2,1,0:T(8,128)S(1)} %get-tuple-element.26.lkv, ...), custom_call_target="tpu_custom_call" | custom-call | tf_op jit(solution)/shard_map/scatter/pallas_call | solution.py:525
  82.8 1.2 %emit.1 = (bf16[256,2560]{1,0:T(8,128)(2,1)}, bf16[256,512]{1,0:T(8,128)(2,1)}, bf16[256,512]{1,0:T(8,128)(2,1)}) custom-call(bf16[256,2560]{1,0:T(8,128)(2,1)S(1)} %get-tuple-element.32.refs_0_, bf16[256,512]{1,0:T(8,128)(2,1)S(1)} %get-tuple-element.33.refs_1_, bf16[256,512]{1,0:T(8,128)(2,1)S(1)} %get-tuple-element.34.refs_2_), custom_call_target="tpu_custom_call" | custom-call | tf_op jit(solution)/shard_map/emit/pallas_call | solution.py:549
Async XLA Ops:
  2.5 0.7 copy-start

commit v4 on v3

--- a/solution.py
+++ b/solution.py
@@ -290,7 +290,7 @@
                 head_copy(h, n, t).wait_send()
 
 
-def attend_kernel(order, ks, vs, qs, dos, stats, acc, dqt, inverse, jq, iq, ik):
+def attend_kernel(order, ks, vs, qs, dos, stats, acc, dqt, inverse, jq, iq, ik, iodd, kodd):
     a, b, sa, sb = place()
     core = lax.rem(lax.axis_index("island"), 2)
     ends = doc_ends(order)
@@ -303,7 +303,8 @@
     acc[...] = jnp.zeros_like(acc)
     dqt[...] = jnp.zeros_like(dqt)
 
-    def plan(i, p):
+    def plan(i, carry):
+        p, odd = carry
         j = order[(i // 2 * sa + b * sb) * 2 + lax.rem(i, 2)]
         jq[i] = j
         low = doc_start(j * BLK, ends) // BLK
@@ -315,21 +316,25 @@
             return p + (y + core * (x - y) != b).astype(jnp.int32)
 
         q = lax.fori_loop(low, j, look, p)
-        ik[q] = -1
-        q = q + lax.rem(q, 2)
+        rest = lax.rem(q, 2)
+        iodd[odd] = i
+        kodd[odd] = ik[jnp.maximum(q - 1, 0)]
+        q = q - rest
 
         def name(t, carry):
             iq[t] = i
             return carry
 
         lax.fori_loop(p // 2, q // 2, name, 0)
-        return q
-
-    total = lax.fori_loop(0, NLOC, plan, 0) // 2
-    def front(t):
-        i = iq[t]
-        c = [ik[2 * t + u] for u in range(2)]
-        at = [span(inverse[jnp.maximum(n, 0)], BLK) for n in c]
+        return q, odd + rest
+
+    total, odd = lax.fori_loop(0, NLOC, plan, (0, 0))
+    total = total // 2
+
+    def front(t, size):
+        i = iq[t] if size == 2 else iodd[t]
+        c = [ik[2 * t + u] for u in range(2)] if size == 2 else [kodd[t]]
+        at = [span(inverse[n], BLK) for n in c]
         keys = jnp.concatenate([ks[n, :] for n in at])
         values = jnp.concatenate([vs[n, :] for n in at])
         q = qs[i // 2, :, span(lax.rem(i, 2), BLK), :].reshape(QW, HD)
@@ -337,37 +342,40 @@
         st = stats[i]
         pos = jq[i] * BLK + lax.broadcasted_iota(jnp.int32, (1, BLK), 1)
         iota = lax.broadcasted_iota(jnp.int32, (BLK, BLK), 0)
-        kpos = jnp.concatenate([n * BLK + iota for n in c])
-        mask = (kpos >= doc_start(pos, ends)) & (kpos <= pos)
+        mask = jnp.concatenate([n * BLK + iota for n in c]) >= doc_start(pos, ends)
         p, d = weigh(keys, values, q, do, st[0:1], st[1:2], mask)
         return i, at, keys, q, do, p, d
 
     def back(i, at, keys, q, do, p, d):
         gv = jnp.dot(p, do, preferred_element_type=jnp.float32)
         gk = jnp.dot(d, q, preferred_element_type=jnp.float32)
-        for n in range(2):
+        for n in range(len(at)):
             acc[at[n], HD : 2 * HD] += gv[n * BLK : (n + 1) * BLK]
             acc[at[n], 0:HD] += gk[n * BLK : (n + 1) * BLK]
         dqt[i] += lax.dot_general(keys, d, TN, preferred_element_type=jnp.float32)
 
-    def group(first, size):
-        held = front(first)
-        for u in range(1, size):
-            following = front(first + u)
+    def group(first, count, size):
+        held = front(first, size)
+        for u in range(1, count):
+            following = front(first + u, size)
             back(*held)
             held = following
         back(*held)
 
-    def step(s, carry):
-        group(s * DEEP, DEEP)
-        return carry
-
-    def single(s, carry):
-        group(s, 1)
-        return carry
-
-    lax.fori_loop(0, total // DEEP, step, 0)
-    lax.fori_loop(total // DEEP * DEEP, total, single, 0)
+    def run(total, deep, size):
+        def many(s, carry):
+            group(s * deep, deep, size)
+            return carry
+
+        def single(s, carry):
+            group(s, 1, size)
+            return carry
+
+        lax.fori_loop(0, total // deep, many, 0)
+        lax.fori_loop(total // deep * deep, total, single, 0)
+
+    run(total, DEEP, 2)
+    run(odd, 3, 1)
 
 
 def scatter_kernel(
@@ -380,65 +388,77 @@
     def dev(aa, bb):
         return {"seq": aa * sa + bb * sb}
 
-    def slot(aa, bb):
-        return span(aa * sa + bb * sb, ROWS)
-
     up, down = dev(a, B[1]), dev(a, B[3])
     toward = (up, up, down, down)
+    other = (down, down, up, up)
     next_b = (B[1], B[1], B[3], B[3])
     other_b = (B[3], B[3], B[1], B[1])
-    other = (down, down, up, up)
-    for t in range(SIDE):
-        sent[t] = acc[slot(A[t], B[2]), :].astype(jnp.bfloat16)
+
+    def rows_of(bb, t, u):
+        return acc[pl.ds(pl.multiple_of((A[t] * sa + bb * sb) * ROWS + u * BLK, BLK), BLK), :]
+
+    order = [(t, u) for ts in ((2, 1), (3, 0)) for u in range(2) for t in ts]
+    for t, u in order:
+        sent[0, t, u] = rows_of(B[2], t, u).astype(jnp.bfloat16)
     greet([dev(A[1], b), dev(A[3], b), dev(A[2], b), up, down])
     wires = Wires(ssem, rsem)
-    through = [wires.send(sent.at[t], thr.at[t], toward[t]) for t in range(SIDE)]
-    plain = [None] * SIDE
-    for t in (0, 2, 1, 3):
-        sent[SIDE + t] = acc[slot(A[t], other_b[t]), :].astype(jnp.bfloat16)
-        plain[t] = wires.send(sent.at[SIDE + t], got.at[1 if t < 2 else 0, t], other[t])
-
-    def finish(t):
+    through, plain, summed = {}, {}, {}
+    for t, u in order:
+        through[t, u] = wires.send(sent.at[0, t, u], thr.at[t, u], toward[t])
+    for t, u in order:
+        sent[1, t, u] = rows_of(other_b[t], t, u).astype(jnp.bfloat16)
+        plain[t, u] = wires.send(sent.at[1, t, u], got.at[1 if t < 2 else 0, t, u], other[t])
+
+    heads, copies, last = [], [], []
+
+    def give(t):
         for u in range(2):
             m = 2 * A[t] + u
             for h in range(GROUP):
                 part = slice(h * BLK, (h + 1) * BLK)
                 g = (dqt[m, :, part] + (l0, l1, l2, l3, l4)[h][m]) * SCALE
-                dqs[t, u * BLK : (u + 1) * BLK, part] = g.T.astype(jnp.bfloat16)
-
-    heads = []
-    for t in (2, 1, 3):
-        finish(t)
-        heads.append(wires.send(dqs.at[t], dq.at[:, span(a, QW)], dev(A[t], b)))
-    summed = [None] * SIDE
-    for t in (0, 2, 1, 3):
-        through[t].wait_recv()
-        total = acc[slot(A[t], next_b[t]), :] + thr[t].astype(jnp.float32)
-        mid[t] = total.astype(jnp.bfloat16)
-        summed[t] = wires.send(mid.at[t], got.at[0 if t < 2 else 1, t], toward[t])
-    finish(0)
-    copies = [pltpu.make_async_copy(dqs.at[0], dq.at[:, span(a, QW)], lsem.at[0])]
-    copies[0].start()
-    last = []
-    for t in (2, 1, 3, 0):
-        plain[t].wait_recv()
-        summed[t].wait_recv()
-        own = lkv[pl.ds(2 * A[t], 2)].reshape(ROWS, 2 * HD)
-        total = own + got[0, t].astype(jnp.float32) + got[1, t].astype(jnp.float32)
-        grads[t, :, 0:HD] = (total[:, 0:HD] * SCALE).astype(jnp.bfloat16)
-        grads[t, :, HD : 2 * HD] = total[:, HD : 2 * HD].astype(jnp.bfloat16)
+                dqs[t, u, :, part] = g.T.astype(jnp.bfloat16)
+            dst = dq.at[pl.ds(u * BLK, BLK), span(a, QW)]
+            if t:
+                heads.append(wires.send(dqs.at[t, u], dst, dev(A[t], b)))
+            else:
+                copies.append(pltpu.make_async_copy(dqs.at[t, u], dst, lsem.at[u]))
+                copies[-1].start()
+
+    def pass_on(t, u):
+        through[t, u].wait_recv()
+        total = rows_of(next_b[t], t, u) + thr[t, u].astype(jnp.float32)
+        mid[t, u] = total.astype(jnp.bfloat16)
+        summed[t, u] = wires.send(mid.at[t, u], got.at[0 if t < 2 else 1, t, u], toward[t])
+
+    give(2)
+    give(1)
+    for t, u in order[:4]:
+        pass_on(t, u)
+    give(3)
+    for t, u in order[4:]:
+        pass_on(t, u)
+    give(0)
+    for t, u in order:
+        plain[t, u].wait_recv()
+        summed[t, u].wait_recv()
+        total = lkv[2 * A[t] + u] + got[0, t, u].astype(jnp.float32) + got[1, t, u].astype(jnp.float32)
+        grads[t, u, :, 0:HD] = (total[:, 0:HD] * SCALE).astype(jnp.bfloat16)
+        grads[t, u, :, HD : 2 * HD] = total[:, HD : 2 * HD].astype(jnp.bfloat16)
         for n, d in enumerate((dk, dv)):
-            src = grads.at[t, :, pl.ds(n * HD, HD)]
+            src = grads.at[t, u, :, pl.ds(n * HD, HD)]
+            dst = d.at[pl.ds(u * BLK, BLK), span(a, HD)]
             if t:
-                last.append(wires.send(src, d.at[:, span(a, HD)], dev(A[t], b)))
+                last.append(wires.send(src, dst, dev(A[t], b)))
             else:
-                copy = pltpu.make_async_copy(src, d.at[:, span(a, HD)], lsem.at[1 + n])
-                copy.start()
-                copies.append(copy)
+                copies.append(pltpu.make_async_copy(src, dst, lsem.at[2 + 2 * u + n]))
+                copies[-1].start()
     for copy in heads + last:
         copy.wait()
-    for copy in through + plain + summed:
-        copy.wait_send()
+    for key in order:
+        through[key].wait_send()
+        plain[key].wait_send()
+        summed[key].wait_send()
     for copy in copies:
         copy.wait()
 
@@ -514,6 +534,8 @@
             pltpu.SMEM((NLOC,), jnp.int32),
             pltpu.SMEM((128,), jnp.int32),
             pltpu.SMEM((256,), jnp.int32),
+            pltpu.SMEM((2 * NLOC,), jnp.int32),
+            pltpu.SMEM((2 * NLOC,), jnp.int32),
         ],
         compiler_params=pltpu.CompilerParams(vmem_limit_bytes=28 * MIB),
         name="attend",
@@ -521,22 +543,22 @@
 
 
 def scatter_call(acc, dqt, lkv, *ldq):
-    piece = (SIDE, ROWS, 2 * HD)
+    piece = (SIDE, 2, BLK, 2 * HD)
     return pl.pallas_call(
         scatter_kernel,
         out_shape=shapes(((ROWS, SIDE * QW), BF), ((ROWS, SIDE * HD), BF), ((ROWS, SIDE * HD), BF)),
         in_specs=[VMEM] * 8,
         out_specs=[ANY] * 3,
         scratch_shapes=[
-            pltpu.VMEM((2 * SIDE, ROWS, 2 * HD), BF),
+            pltpu.VMEM((2,) + piece, BF),
             pltpu.VMEM(piece, BF),
             pltpu.VMEM(piece, BF),
             pltpu.VMEM((2,) + piece, BF),
             pltpu.VMEM(piece, BF),
-            pltpu.VMEM((SIDE, ROWS, QW), BF),
-            pltpu.SemaphoreType.DMA((24,)),
-            pltpu.SemaphoreType.DMA((24,)),
-            pltpu.SemaphoreType.DMA((4,)),
+            pltpu.VMEM((SIDE, 2, BLK, QW), BF),
+            pltpu.SemaphoreType.DMA((48,)),
+            pltpu.SemaphoreType.DMA((48,)),
+            pltpu.SemaphoreType.DMA((8,)),
         ],
         compiler_params=pltpu.CompilerParams(
             collective_id=2, has_side_effects=True, vmem_limit_bytes=28 * MIB

time: 84.4 us -> 80.6 us (0.955)
  the two profiles are of different devices: /device:TPU:98 before, /device:TPU:0 now
where the time goes in v4:
time: 80.6 us; the launch traced here: 79.9 us
  Pallas kernels  76.5 us (95%)
  other arithmetic  1.82 us (2%)
  between operations  0.83 us (1%)
    pallas_call x1, Pallas kernels, gather_call(): pl.pallas_call(gather_kernel, out_shape=shapes(((TOKENS, HD), BF), ((TOKE...  37.2 us
    pallas_call x1, Pallas kernels, scatter_call(): pl.pallas_call(scatter_kernel, out_shape=shapes(((ROWS, SIDE * QW), BF),...  26.1 us
    pallas_call x1, Pallas kernels, attend_call(): pl.pallas_call(attend_kernel, out_shape=shapes(((TOKENS, 2 * HD), F32), (...  11.9 us

profile of v4, /device:TPU:0, one launch (start us, length us, event | category | flops | bytes accessed | tf_op | source)
XLA Modules:
  0.0 79.9 jit_solution(5338467323617889523)
XLA Ops:
  0.6 0.7 pad_add_fusion.facts_ref.order
  1.4 1.1 %pad_maximum_fusion.kv_ref = bf16[256,1024]{1,0:T(8,128)(2,1)S(1)} fusion(bf16[256,512]{1,0:T(8,128)(2,1)} %param.10, bf16[256,512]{1,0:T(8,128)(2,1)} %param.9), kind=kLoop, calls=%fused_computation | loop fusion | flops 1048576 | bytes 1048576 | tf_op jit(solution)/shard_map/concatenate | solution.py:584
  2.5 0.0 copy-start
  2.5 0.7 copy-done
  3.2 37.2 %gather.1 = (bf16[4096,128]{1,0:T(8,128)(2,1)S(1)}, bf16[4096,128]{1,0:T(8,128)(2,1)S(1)}, bf16[4,5,256,128]{3,2,1,0:T(8,128)(2,1)S(1)}, bf16[4,5,256,128]{3,2,1...) custom-call(s32[36]{0:T(128)S(1)} %pad_add_fusion.facts_ref.order, ...), custom_call_target="tpu_custom_call" | custom-call | tf_op jit(solution)/shard_map/gather/pallas_call | solution.py:490
  40.4 11.9 %attend.1 = (f32[4096,256]{1,0:T(8,128)S(1)}, f32[8,128,640]{2,1,0:T(8,128)S(1)}) custom-call(s32[36]{0:T(128)S(1)} %pad_add_fusion.facts_ref.order, bf16[4096,128]{1,0:T(8,128)(2,1)S(1)} %get-tuple-element.19.ks, bf16[4096,128]{1,0:T(8,128)(2,1)S(1)} %get-tuple-element.20.vs, bf16[4,5,256,128]{3,2,1,0:T(8,128)(2,1)S(1)} %get-tuple-element.21.qs, ...), custom_call_target="tpu_custom_call" | custom-call | tf_op jit(solution)/shard_map/attend/pallas_call | solution.py:527
  52.4 26.1 %scatter.1 = (bf16[256,2560]{1,0:T(8,128)(2,1)S(1)}, bf16[256,512]{1,0:T(8,128)(2,1)S(1)}, bf16[256,512]{1,0:T(8,128)(2,1)S(1)}) custom-call(f32[4096,256]{1,0:T(8,128)S(1)} %get-tuple-element.24.acc, f32[8,128,640]{2,1,0:T(8,128)S(1)} %get-tuple-element.25.dqt, f32[8,128,256]{2,1,0:T(8,128)S(1)} %get-tuple-element.26.lkv, ...), custom_call_target="tpu_custom_call" | custom-call | tf_op jit(solution)/shard_map/scatter/pallas_call | solution.py:547
  78.5 1.2 %emit.1 = (bf16[256,2560]{1,0:T(8,128)(2,1)}, bf16[256,512]{1,0:T(8,128)(2,1)}, bf16[256,512]{1,0:T(8,128)(2,1)}) custom-call(bf16[256,2560]{1,0:T(8,128)(2,1)S(1)} %get-tuple-element.32.refs_0_, bf16[256,512]{1,0:T(8,128)(2,1)S(1)} %get-tuple-element.33.refs_1_, bf16[256,512]{1,0:T(8,128)(2,1)S(1)} %get-tuple-element.34.refs_2_), custom_call_target="tpu_custom_call" | custom-call | tf_op jit(solution)/shard_map/emit/pallas_call | solution.py:571
Async XLA Ops:
  2.5 0.7 copy-start

commit v5 on v4

--- a/solution.py
+++ b/solution.py
@@ -16,6 +16,7 @@
 GROUP = 5
 QW = GROUP * HD
 TOKENS = 4096
+MOST = 2048
 NBLK = 32
 PAIR = 2 * BLK
 NLOC = 2 * SIDE
@@ -290,32 +291,28 @@
                 head_copy(h, n, t).wait_send()
 
 
-def attend_kernel(order, ks, vs, qs, dos, stats, acc, dqt, inverse, jq, iq, ik, iodd, kodd):
+def attend_kernel(order, ks, vs, qs, dos, stats, acc, dqt, inverse, far, jq, iq, ik, iodd, kodd):
     a, b, sa, sb = place()
     core = lax.rem(lax.axis_index("island"), 2)
     ends = doc_ends(order)
 
-    def invert(n, carry):
+    for n in range(NBLK):
+        x, y = n // 2 % SIDE, n // 2 // SIDE
         inverse[order[n]] = n
-        return carry
-
-    lax.fori_loop(0, NBLK, invert, 0, unroll=4)
-    acc[...] = jnp.zeros_like(acc)
-    dqt[...] = jnp.zeros_like(dqt)
-
+        far[order[n]] = (y + core * (x - y) != b).astype(jnp.int32)
     def plan(i, carry):
         p, odd = carry
+        acc[span(i, TOKENS // NLOC), :] = jnp.zeros((TOKENS // NLOC, 2 * HD), jnp.float32)
+        dqt[i] = jnp.zeros((HD, QW), jnp.float32)
         j = order[(i // 2 * sa + b * sb) * 2 + lax.rem(i, 2)]
         jq[i] = j
         low = doc_start(j * BLK, ends) // BLK
 
-        def look(c, p):
-            seq = inverse[c] // 2
-            x, y = lax.rem(seq, SIDE), seq // SIDE
-            ik[p] = c
-            return p + (y + core * (x - y) != b).astype(jnp.int32)
-
-        q = lax.fori_loop(low, j, look, p)
+        q = p
+        for n in range(1, MOST // BLK + 1):
+            c = jnp.maximum(j - n, 0)
+            ik[q] = c
+            q = q + jnp.where(j - n >= low, far[c], 0)
         rest = lax.rem(q, 2)
         iodd[odd] = i
         kodd[odd] = ik[jnp.maximum(q - 1, 0)]
@@ -531,6 +528,7 @@
         out_specs=[VMEM, VMEM],
         scratch_shapes=[
             pltpu.SMEM((NBLK,), jnp.int32),
+            pltpu.SMEM((NBLK,), jnp.int32),
             pltpu.SMEM((NLOC,), jnp.int32),
             pltpu.SMEM((128,), jnp.int32),
             pltpu.SMEM((256,), jnp.int32),

time: 80.6 us -> 80.9 us (level)
  the two profiles are of different devices: /device:TPU:0 before, /device:TPU:34 now
where the time goes in v5:
time: 80.9 us; the launch traced here: 80.7 us
  Pallas kernels  77.3 us (96%)
  other arithmetic  1.82 us (2%)
  between operations  0.83 us (1%)
    pallas_call x1, Pallas kernels, gather_call(): pl.pallas_call(gather_kernel, out_shape=shapes(((TOKENS, HD), BF), ((TOKE...  35.4 us
    pallas_call x1, Pallas kernels, scatter_call(): pl.pallas_call(scatter_kernel, out_shape=shapes(((ROWS, SIDE * QW), BF),...  33 us
    pallas_call x1, Pallas kernels, attend_call(): pl.pallas_call(attend_kernel, out_shape=shapes(((TOKENS, 2 * HD), F32), (...  7.69 us

profile of v5, /device:TPU:34, one launch (start us, length us, event | category | flops | bytes accessed | tf_op | source)
XLA Modules:
  0.0 80.7 jit_solution(15077091019358912516)
XLA Ops:
  0.6 0.7 pad_add_fusion.facts_ref.order
  1.4 1.1 %pad_maximum_fusion.kv_ref = bf16[256,1024]{1,0:T(8,128)(2,1)S(1)} fusion(bf16[256,512]{1,0:T(8,128)(2,1)} %param.10, bf16[256,512]{1,0:T(8,128)(2,1)} %param.9), kind=kLoop, calls=%fused_computation | loop fusion | flops 1048576 | bytes 1048576 | tf_op jit(solution)/shard_map/concatenate | solution.py:582
  2.5 0.0 copy-start
  2.5 0.7 copy-done
  3.2 35.4 %gather.1 = (bf16[4096,128]{1,0:T(8,128)(2,1)S(1)}, bf16[4096,128]{1,0:T(8,128)(2,1)S(1)}, bf16[4,5,256,128]{3,2,1,0:T(8,128)(2,1)S(1)}, bf16[4,5,256,128]{3,2,1...) custom-call(s32[36]{0:T(128)S(1)} %pad_add_fusion.facts_ref.order, ...), custom_call_target="tpu_custom_call" | custom-call | tf_op jit(solution)/shard_map/gather/pallas_call | solution.py:487
  38.6 7.7 %attend.1 = (f32[4096,256]{1,0:T(8,128)S(1)}, f32[8,128,640]{2,1,0:T(8,128)S(1)}) custom-call(s32[36]{0:T(128)S(1)} %pad_add_fusion.facts_ref.order, bf16[4096,128]{1,0:T(8,128)(2,1)S(1)} %get-tuple-element.19.ks, bf16[4096,128]{1,0:T(8,128)(2,1)S(1)} %get-tuple-element.20.vs, bf16[4,5,256,128]{3,2,1,0:T(8,128)(2,1)S(1)} %get-tuple-element.21.qs, ...), custom_call_target="tpu_custom_call" | custom-call | tf_op jit(solution)/shard_map/attend/pallas_call | solution.py:524
  46.3 33.0 %scatter.1 = (bf16[256,2560]{1,0:T(8,128)(2,1)S(1)}, bf16[256,512]{1,0:T(8,128)(2,1)S(1)}, bf16[256,512]{1,0:T(8,128)(2,1)S(1)}) custom-call(f32[4096,256]{1,0:T(8,128)S(1)} %get-tuple-element.24.acc, f32[8,128,640]{2,1,0:T(8,128)S(1)} %get-tuple-element.25.dqt, f32[8,128,256]{2,1,0:T(8,128)S(1)} %get-tuple-element.26.lkv, ...), custom_call_target="tpu_custom_call" | custom-call | tf_op jit(solution)/shard_map/scatter/pallas_call | solution.py:545
  79.3 1.2 %emit.1 = (bf16[256,2560]{1,0:T(8,128)(2,1)}, bf16[256,512]{1,0:T(8,128)(2,1)}, bf16[256,512]{1,0:T(8,128)(2,1)}) custom-call(bf16[256,2560]{1,0:T(8,128)(2,1)S(1)} %get-tuple-element.32.refs_0_, bf16[256,512]{1,0:T(8,128)(2,1)S(1)} %get-tuple-element.33.refs_1_, bf16[256,512]{1,0:T(8,128)(2,1)S(1)} %get-tuple-element.34.refs_2_), custom_call_target="tpu_custom_call" | custom-call | tf_op jit(solution)/shard_map/emit/pallas_call | solution.py:569
Async XLA Ops:
  2.5 0.7 copy-start

commit v6 on v5

--- a/solution.py
+++ b/solution.py
@@ -430,9 +430,9 @@
 
     give(2)
     give(1)
+    give(3)
     for t, u in order[:4]:
         pass_on(t, u)
-    give(3)
     for t, u in order[4:]:
         pass_on(t, u)
     give(0)

time: 80.9 us -> 80.2 us (level)
  the two profiles are of different devices: /device:TPU:34 before, /device:TPU:0 now
where the time goes in v6:
time: 80.2 us; the launch traced here: 80.6 us
  Pallas kernels  77.3 us (96%)
  other arithmetic  1.82 us (2%)
  between operations  0.83 us (1%)
    pallas_call x1, Pallas kernels, gather_call(): pl.pallas_call(gather_kernel, out_shape=shapes(((TOKENS, HD), BF), ((TOKE...  37.2 us
    pallas_call x1, Pallas kernels, scatter_call(): pl.pallas_call(scatter_kernel, out_shape=shapes(((ROWS, SIDE * QW), BF),...  24.3 us
    pallas_call x1, Pallas kernels, attend_call(): pl.pallas_call(attend_kernel, out_shape=shapes(((TOKENS, 2 * HD), F32), (...  14.5 us

profile of v6, /device:TPU:0, one launch (start us, length us, event | category | flops | bytes accessed | tf_op | source)
XLA Modules:
  0.0 80.6 jit_solution(12937656181641715952)
XLA Ops:
  0.6 0.7 pad_add_fusion.facts_ref.order
  1.4 1.1 %pad_maximum_fusion.kv_ref = bf16[256,1024]{1,0:T(8,128)(2,1)S(1)} fusion(bf16[256,512]{1,0:T(8,128)(2,1)} %param.10, bf16[256,512]{1,0:T(8,128)(2,1)} %param.9), kind=kLoop, calls=%fused_computation | loop fusion | flops 1048576 | bytes 1048576 | tf_op jit(solution)/shard_map/concatenate | solution.py:582
  2.5 0.0 copy-start
  2.5 0.7 copy-done
  3.2 37.2 %gather.1 = (bf16[4096,128]{1,0:T(8,128)(2,1)S(1)}, bf16[4096,128]{1,0:T(8,128)(2,1)S(1)}, bf16[4,5,256,128]{3,2,1,0:T(8,128)(2,1)S(1)}, bf16[4,5,256,128]{3,2,1...) custom-call(s32[36]{0:T(128)S(1)} %pad_add_fusion.facts_ref.order, ...), custom_call_target="tpu_custom_call" | custom-call | tf_op jit(solution)/shard_map/gather/pallas_call | solution.py:487
  40.4 14.5 %attend.1 = (f32[4096,256]{1,0:T(8,128)S(1)}, f32[8,128,640]{2,1,0:T(8,128)S(1)}) custom-call(s32[36]{0:T(128)S(1)} %pad_add_fusion.facts_ref.order, bf16[4096,128]{1,0:T(8,128)(2,1)S(1)} %get-tuple-element.19.ks, bf16[4096,128]{1,0:T(8,128)(2,1)S(1)} %get-tuple-element.20.vs, bf16[4,5,256,128]{3,2,1,0:T(8,128)(2,1)S(1)} %get-tuple-element.21.qs, ...), custom_call_target="tpu_custom_call" | custom-call | tf_op jit(solution)/shard_map/attend/pallas_call | solution.py:524
  54.9 24.3 %scatter.1 = (bf16[256,2560]{1,0:T(8,128)(2,1)S(1)}, bf16[256,512]{1,0:T(8,128)(2,1)S(1)}, bf16[256,512]{1,0:T(8,128)(2,1)S(1)}) custom-call(f32[4096,256]{1,0:T(8,128)S(1)} %get-tuple-element.24.acc, f32[8,128,640]{2,1,0:T(8,128)S(1)} %get-tuple-element.25.dqt, f32[8,128,256]{2,1,0:T(8,128)S(1)} %get-tuple-element.26.lkv, ...), custom_call_target="tpu_custom_call" | custom-call | tf_op jit(solution)/shard_map/scatter/pallas_call | solution.py:545
  79.2 1.2 %emit.1 = (bf16[256,2560]{1,0:T(8,128)(2,1)}, bf16[256,512]{1,0:T(8,128)(2,1)}, bf16[256,512]{1,0:T(8,128)(2,1)}) custom-call(bf16[256,2560]{1,0:T(8,128)(2,1)S(1)} %get-tuple-element.32.refs_0_, bf16[256,512]{1,0:T(8,128)(2,1)S(1)} %get-tuple-element.33.refs_1_, bf16[256,512]{1,0:T(8,128)(2,1)S(1)} %get-tuple-element.34.refs_2_), custom_call_target="tpu_custom_call" | custom-call | tf_op jit(solution)/shard_map/emit/pallas_call | solution.py:569
Async XLA Ops:
  2.5 0.7 copy-start

commit v7 on v6

--- a/solution.py
+++ b/solution.py
@@ -435,7 +435,6 @@
         pass_on(t, u)
     for t, u in order[4:]:
         pass_on(t, u)
-    give(0)
     for t, u in order:
         plain[t, u].wait_recv()
         summed[t, u].wait_recv()
@@ -450,6 +449,7 @@
             else:
                 copies.append(pltpu.make_async_copy(src, dst, lsem.at[2 + 2 * u + n]))
                 copies[-1].start()
+    give(0)
     for copy in heads + last:
         copy.wait()
     for key in order:

time: 80.2 us -> 80.1 us (level); the launches traced: 80.6 us -> 78.9 us
  Pallas kernels: 77.3 us -> 75.5 us
    pallas_call x1, Pallas kernels: 14.5 us -> 13 us  [attend_call(): pl.pallas_call(attend_kernel, out_shape=shapes(((TOKENS, 2 * HD), F32), (...]
where the time goes in v7:
time: 80.1 us; the launch traced here: 78.9 us
  Pallas kernels  75.5 us (94%)
  other arithmetic  1.82 us (2%)
  between operations  0.83 us (1%)
    pallas_call x1, Pallas kernels, gather_call(): pl.pallas_call(gather_kernel, out_shape=shapes(((TOKENS, HD), BF), ((TOKE...  37.2 us
    pallas_call x1, Pallas kernels, scatter_call(): pl.pallas_call(scatter_kernel, out_shape=shapes(((ROWS, SIDE * QW), BF),...  24.1 us
    pallas_call x1, Pallas kernels, attend_call(): pl.pallas_call(attend_kernel, out_shape=shapes(((TOKENS, 2 * HD), F32), (...  13 us

profile of v7, /device:TPU:0, one launch (start us, length us, event | category | flops | bytes accessed | tf_op | source)
XLA Modules:
  0.0 78.9 jit_solution(16896077679686434510)
XLA Ops:
  0.6 0.7 pad_add_fusion.facts_ref.order
  1.4 1.1 %pad_maximum_fusion.kv_ref = bf16[256,1024]{1,0:T(8,128)(2,1)S(1)} fusion(bf16[256,512]{1,0:T(8,128)(2,1)} %param.10, bf16[256,512]{1,0:T(8,128)(2,1)} %param.9), kind=kLoop, calls=%fused_computation | loop fusion | flops 1048576 | bytes 1048576 | tf_op jit(solution)/shard_map/concatenate | solution.py:582
  2.5 0.0 copy-start
  2.5 0.7 copy-done
  3.2 37.2 %gather.1 = (bf16[4096,128]{1,0:T(8,128)(2,1)S(1)}, bf16[4096,128]{1,0:T(8,128)(2,1)S(1)}, bf16[4,5,256,128]{3,2,1,0:T(8,128)(2,1)S(1)}, bf16[4,5,256,128]{3,2,1...) custom-call(s32[36]{0:T(128)S(1)} %pad_add_fusion.facts_ref.order, ...), custom_call_target="tpu_custom_call" | custom-call | tf_op jit(solution)/shard_map/gather/pallas_call | solution.py:487
  40.4 13.0 %attend.1 = (f32[4096,256]{1,0:T(8,128)S(1)}, f32[8,128,640]{2,1,0:T(8,128)S(1)}) custom-call(s32[36]{0:T(128)S(1)} %pad_add_fusion.facts_ref.order, bf16[4096,128]{1,0:T(8,128)(2,1)S(1)} %get-tuple-element.19.ks, bf16[4096,128]{1,0:T(8,128)(2,1)S(1)} %get-tuple-element.20.vs, bf16[4,5,256,128]{3,2,1,0:T(8,128)(2,1)S(1)} %get-tuple-element.21.qs, ...), custom_call_target="tpu_custom_call" | custom-call | tf_op jit(solution)/shard_map/attend/pallas_call | solution.py:524
  53.4 24.1 %scatter.1 = (bf16[256,2560]{1,0:T(8,128)(2,1)S(1)}, bf16[256,512]{1,0:T(8,128)(2,1)S(1)}, bf16[256,512]{1,0:T(8,128)(2,1)S(1)}) custom-call(f32[4096,256]{1,0:T(8,128)S(1)} %get-tuple-element.24.acc, f32[8,128,640]{2,1,0:T(8,128)S(1)} %get-tuple-element.25.dqt, f32[8,128,256]{2,1,0:T(8,128)S(1)} %get-tuple-element.26.lkv, ...), custom_call_target="tpu_custom_call" | custom-call | tf_op jit(solution)/shard_map/scatter/pallas_call | solution.py:545
  77.5 1.2 %emit.1 = (bf16[256,2560]{1,0:T(8,128)(2,1)}, bf16[256,512]{1,0:T(8,128)(2,1)}, bf16[256,512]{1,0:T(8,128)(2,1)}) custom-call(bf16[256,2560]{1,0:T(8,128)(2,1)S(1)} %get-tuple-element.32.refs_0_, bf16[256,512]{1,0:T(8,128)(2,1)S(1)} %get-tuple-element.33.refs_1_, bf16[256,512]{1,0:T(8,128)(2,1)S(1)} %get-tuple-element.34.refs_2_), custom_call_target="tpu_custom_call" | custom-call | tf_op jit(solution)/shard_map/emit/pallas_call | solution.py:569
Async XLA Ops:
  2.5 0.7 copy-start
